TPU v7x, 256 devices: a whole 4x4x8 slice. The times are simulated.
256 devices in a mesh: dp: 16 (over y, z_lo, core), seq: 16 (over x, z_hi).
Axes of the slice: x: 4, y: 4, z: 8 (z_hi: 4, z_lo: 2; z = z_hi * 2 + z_lo), core: 2. Of those that a mesh axis runs over, the one named last changes fastest.
Arguments:
- x1_pixels: bfloat16 [16, 16, 256, 1152], P('dp', None, 'seq'), may hold values from -400 to 400, as said below
- dout_frames: bfloat16 [16, 16, 256, 1152], P('dp', 'seq'), may hold values from -6 to 6
- w_qkv: bfloat16 [1152, 3456], replicated, may hold values from -0.1875 to 0.1875
- w_out: bfloat16 [1152, 1152], replicated, may hold values from -0.1875 to 0.1875
Outputs:
- d_x1: bfloat16 [16, 16, 256, 1152], P('dp', 'seq')
- g_qkv: float32 [1152, 3456], P('dp', 'seq')
- g_out: float32 [1152, 1152], P('dp', 'seq')
Inputs may be any that keep to these rules, and one draw needn't show every extreme that they name: `x1_pixels`: features of a token have unlike scales.
All inputs are finite; a program needn't handle non-finite values.
Results may differ from a plain program's by a relative error of at most 0.0072.
The roundings to bfloat16 on the way count: a program that leaves them out, or rounds other values in their place, can miss the bound.
Values may be sent and summed in bfloat16 or wider, within the bound.
A program may use at most 192 MiB of HBM per device.

v0:
```python
import math

import jax
import jax.numpy as jnp
from jax import lax
from jax.sharding import PartitionSpec as P

HEADS = 16


EPS = 1e-06


def centre_rows(inputs):
    values = inputs.astype(jnp.float32)
    centred = values - jnp.mean(values, axis=-1, keepdims=True)
    inverse = lax.rsqrt(jnp.mean(centred * centred, axis=-1, keepdims=True) + EPS)
    return (centred * inverse, inverse)


def head_scale(values):
    return values * lax.rsqrt(jnp.mean(values * values, axis=-1, keepdims=True) + EPS)


def pair_scale(first, second):
    return (head_scale(first), head_scale(second))


def batched(form, left, right):
    return jnp.einsum(form, left, right, preferred_element_type=jnp.float32)


def temporal_terms(inputs, upstream, w_qkv, w_out):
    lead = inputs.shape[:3]
    width = inputs.shape[3]
    tokens_here = lead[0] * lead[1] * lead[2]
    head_size = width // HEADS
    split_shape = lead + (HEADS, head_size)
    standard, inverse = centre_rows(inputs)
    normed = standard.astype(jnp.bfloat16).reshape(tokens_here, width)
    projected = jnp.dot(normed, w_qkv, preferred_element_type=jnp.float32)
    query = projected[:, :width].reshape(split_shape)
    keys_raw = projected[:, width : 2 * width].reshape(split_shape)
    values_raw = projected[:, 2 * width :].reshape(split_shape)
    (query_n, keys_n), norm_back = jax.vjp(pair_scale, query, keys_raw)
    query_b = query_n.astype(jnp.bfloat16)
    keys_b = keys_n.astype(jnp.bfloat16)
    values_b = values_raw.astype(jnp.bfloat16)
    factor = head_size ** (-0.5)
    scores = batched("bfphd,bgphd->bphfg", query_b, keys_b) * factor
    weights = jnp.exp(scores)
    probs = weights / jnp.sum(weights, axis=-1, keepdims=True)
    probs_b = probs.astype(jnp.bfloat16)
    attended = batched("bphfg,bgphd->bfphd", probs_b, values_b).astype(jnp.bfloat16)
    flat_att = attended.reshape(tokens_here, width)
    flat_up = upstream.reshape(tokens_here, width)
    grad_out = jnp.dot(flat_att.T, flat_up, preferred_element_type=jnp.float32)
    grad_att = (
        jnp.dot(flat_up, w_out.T, preferred_element_type=jnp.float32)
        .astype(jnp.bfloat16)
        .reshape(split_shape)
    )
    grad_probs = batched("bfphd,bgphd->bphfg", grad_att, values_b)
    grad_values = batched("bphfg,bfphd->bgphd", probs_b, grad_att)
    grad_scores = (
        probs * (grad_probs - jnp.sum(probs * grad_probs, axis=-1, keepdims=True)) * factor
    ).astype(jnp.bfloat16)
    grad_qn = batched("bphfg,bgphd->bfphd", grad_scores, keys_b)
    grad_kn = batched("bphfg,bfphd->bgphd", grad_scores, query_b)
    grad_query, grad_keys = norm_back((grad_qn, grad_kn))
    grad_proj = jnp.concatenate(
        [
            grad_query.reshape(tokens_here, width),
            grad_keys.reshape(tokens_here, width),
            grad_values.reshape(tokens_here, width),
        ],
        axis=1,
    ).astype(jnp.bfloat16)
    grad_qkv = jnp.dot(normed.T, grad_proj, preferred_element_type=jnp.float32)
    grad_normed = jnp.dot(grad_proj, w_qkv.T, preferred_element_type=jnp.float32).reshape(
        lead + (width,)
    )
    branch = inverse * (
        grad_normed
        - jnp.mean(grad_normed, axis=-1, keepdims=True)
        - standard * jnp.mean(grad_normed * standard, axis=-1, keepdims=True)
    )
    return (branch.astype(jnp.bfloat16), grad_qkv, grad_out)


def local(x1_pixels, dout_frames, w_qkv, w_out):
    upstream = lax.all_to_all(dout_frames, "seq", split_axis=2, concat_axis=1, tiled=True)
    branch, grad_qkv, grad_out = temporal_terms(x1_pixels, upstream, w_qkv, w_out)
    returned = lax.all_to_all(branch, "seq", split_axis=1, concat_axis=2, tiled=True)
    d_x1 = (dout_frames.astype(jnp.float32) + returned.astype(jnp.float32)).astype(jnp.bfloat16)
    row_parts = lax.axis_size("dp")
    col_parts = lax.axis_size("seq")
    count = x1_pixels.shape[0] * x1_pixels.shape[1] * x1_pixels.shape[2] * row_parts * col_parts
    factor = 1.0 / math.sqrt(count)
    scaled_qkv = grad_qkv * factor
    scaled_out = grad_out * factor
    row_qkv, row_out = (
        lax.psum_scatter(scaled_qkv, "dp", scatter_dimension=0, tiled=True),
        lax.psum_scatter(scaled_out, "dp", scatter_dimension=0, tiled=True),
    )
    share_qkv, share_out = (
        lax.psum_scatter(row_qkv, "seq", scatter_dimension=1, tiled=True),
        lax.psum_scatter(row_out, "seq", scatter_dimension=1, tiled=True),
    )
    return (d_x1, share_qkv, share_out)


def solution(mesh):
    return jax.shard_map(
        local,
        mesh=mesh,
        in_specs=(P("dp", None, "seq", None), P("dp", "seq", None, None), P(), P()),
        out_specs=(P("dp", "seq", None, None), P("dp", "seq"), P("dp", "seq")),
        check_vma=False,
    )
```

profile of v0, /device:TPU:32, one launch (start us, length us, event | category | flops | bytes accessed | tf_op | source)
XLA Modules:
  0.0 529.8 jit_solution(14868767354120220059)
XLA Ops:
  7.2 3.1 copy.161
  10.8 6.0 %reduce.13 = bf16[256,1152]{1,0:T(8,128)(2,1)} reduce(bf16[256,1,1,1152]{3,2,1,0:T(2,128)(2,1)} %bitcast.72, bf16[]{:T(256)} %broadcast.216), dimensions={1,2}, to_apply=%bitcast.70.reduce_sub_computation | reduce | bytes 1179650
  16.8 2.5 reshape.313
  19.3 10.2 %all-to-all-start = ((bf16[16,2,9216]{2,1,0:T(2,128)(2,1)}), bf16[16,2,9216]{2,1,0:T(2,128)(2,1)}, u32[]{:S(2)}, u32[]{:S(2)}) async-start(bf16[16,2,9216]{2,1,0:T(2,128)(2,1)} %reshape.313), calls=%async_computation | async-start | bytes 1179648 | tf_op jit(solution)/shard_map/all_to_all | solution.py:92
  30.3 6.0 %fusion.67 = f32[256,3456]{1,0:T(8,128)S(1)} fusion(bf16[256,1152]{1,0:T(8,128)(2,1)S(1)} %bitcast.75, bf16[1152,3456]{1,0:T(8,128)(2,1)} %param.6), kind=kOutput, calls=%fused_computation.83 | convolution fusion | flops 2038431744 | bytes 12091392 | tf_op jit(solution)/shard_map/dot_general | solution.py:41
  38.8 4.2 reshape.296
  43.1 2.2 multiply_reduce_fusion.1
  46.0 3.8 reshape.294
  49.8 2.2 multiply_reduce_fusion.2
  52.0 2.1 slice.17
  54.1 3.8 reshape.295
  57.9 3.8 reshape.293
  61.7 3.7 convert_element_type.78
  67.9 5.3 fusion.11
  75.8 2.9 reshape.303
  78.7 3.5 reshape.314
  82.3 4.7 convolution_multiply_fusion.1
  87.1 3.1 convolution_convert_fusion
  90.2 3.1 reshape.298
  94.3 2.7 fusion.17
  99.4 4.7 fusion.34
  104.0 8.8 %fusion.4 = (f32[16,16,16]{0,2,1:T(8,128)S(1)}, f32[16,16,72,16]{2,3,1,0:T(8,128)}) fusion(f32[1,16,16,16,72]{4,3,2,1,0:T(8,128)S(1)} %copy-done.3, f32[16,16,16,16]{2,3,1,0:T(8,128)} %fusion.34, f32[16,16,16]{2,1,0:T(8,128)S(1)} %copy-done.19, f32[16,16,16,16]{2,3,1,0:T(8,128)} %copy-done.14, f32[16,16,16,72]{3,2,1,0:T(8,128)} %reshape.293, ...), kind=kOutput, calls=%fused_computation.13 | convolution fusion | flops 11206671 | bytes 4112384 | tf_op jit(solution)/shard_map/bphfg,bgphd->bfphd/dot_general | solution.py:30
  113.2 3.2 fusion.1
  117.7 3.1 reshape.299
  120.8 8.9 %fusion.3 = (f32[16,16,16]{0,2,1:T(8,128)S(1)}, f32[16,16,72,16]{2,3,1,0:T(8,128)}) fusion(f32[1,16,16,16,72]{4,3,2,1,0:T(8,128)S(1)} %copy-done.2, f32[16,16,16,16]{2,3,1,0:T(8,128)} %fusion.34, f32[16,16,16]{2,1,0:T(8,128)S(1)} %copy-done.20, f32[16,16,16,16]{2,3,1,0:T(8,128)} %copy-done.14, f32[16,16,16,72]{3,2,1,0:T(8,128)} %reshape.295, ...), kind=kOutput, calls=%fused_computation.10 | convolution fusion | flops 11206671 | bytes 4112384 | tf_op jit(solution)/shard_map/bphfg,bfphd->bgphd/dot_general | solution.py:30
  130.1 3.2 fusion.2
  138.1 7.9 %convolution_multiply_fusion = f32[1152,3456]{1,0:T(8,128)} fusion(bf16[256,1152]{1,0:T(8,128)(2,1)S(1)} %bitcast.76, bf16[256,3456]{1,0:T(8,128)(2,1)S(1)} %constant_dynamic-update-slice_fusion), kind=kOutput, calls=%fused_computation.1 | convolution fusion | flops 2042413056 | bytes 18284544 | tf_op jit(solution)/shard_map/dot_general | solution.py:79
  146.1 6.5 %fusion.66 = (f32[256]{0:T(256)S(1)}, f32[256,1152]{1,0:T(8,128)S(1)}) fusion(bf16[256,3456]{1,0:T(8,128)(2,1)} %copy-done.8, bf16[1152,3456]{1,0:T(8,128)(2,1)} %param.6), kind=kOutput, calls=%fused_computation.81 | convolution fusion | flops 2038726400 | bytes 10912768 | tf_op jit(solution)/shard_map/dot_general | solution.py:80
  154.0 2.6 fusion.28
  156.6 9.6 %all-to-all-start.1 = ((bf16[1,16,16,1152]{3,2,0,1:T(8,128)(2,1)}), bf16[1,16,16,1152]{3,2,0,1:T(8,128)(2,1)}, u32[]{:S(2)}, u32[]{:S(2)}) async-start(bf16[1,16,16,1152]{3,2,0,1:T(8,128)(2,1)} %fusion.28), calls=%async_computation.1 | async-start | bytes 1179648 | tf_op jit(solution)/shard_map/all_to_all | solution.py:94
  166.4 175.2 %reduce-scatter.11.cloned.1.call-done = f32[72,3456]{1,0:T(8,128)} async-done(((f32[1152,3456]{1,0:T(8,128)}), f32[72,3456]{1,0:T(8,128)}) %reduce-scatter.11.cloned.1.call-update) | async-done | bytes 995344
  345.5 174.4 %all-reduce.7.cloned.1.call-done = (f32[72,3456]{1,0:T(8,128)}, f32[72,1152]{1,0:T(8,128)}) async-done(((f32[72,3456]{1,0:T(8,128)}, f32[72,1152]{1,0:T(8,128)}), (f32[72,3456]{1,0:T(8,128)}, f32[72,1152]{1,0:T(8,128)})) %all-reduce.7.cloned.1.call-update) | async-done | bytes 1327120
  (88 shorter events, 26.8 us)
Async XLA Ops:
  7.2 79.9 %copy-start = (bf16[1152,1152]{1,0:T(8,128)(2,1)S(1)}, bf16[1152,1152]{1,0:T(8,128)(2,1)}, u32[]{:S(2)}) copy-start(bf16[1152,1152]{1,0:T(8,128)(2,1)} %param.7) | copy-start | bytes 7962628
  10.3 19.2 %copy-start.4 = (bf16[1,16,16,1152]{3,2,1,0:T(8,128)(2,1)S(1)}, bf16[1,16,16,1152]{3,2,1,0:T(8,128)(2,1)}, u32[]{:S(2)}) copy-start(bf16[1,16,16,1152]{3,2,1,0:T(8,128)(2,1)} %param.4) | copy-start | bytes 1769476
  19.3 59.4 %all-to-all-start = ((bf16[16,2,9216]{2,1,0:T(2,128)(2,1)}), bf16[16,2,9216]{2,1,0:T(2,128)(2,1)}, u32[]{:S(2)}, u32[]{:S(2)}) async-start(bf16[16,2,9216]{2,1,0:T(2,128)(2,1)} %reshape.313), calls=%async_computation | async-start | bytes 1179648 | tf_op jit(solution)/shard_map/all_to_all | solution.py:92
  29.5 136.9 %reduce-scatter.13.cloned.1.call-start = ((), (), s32[]{:S(2)}) async-start(), calls=%async_computation.5 | async-start | bytes 5640192
  30.3 6.0 %copy-start.10 = (bf16[1,16,16,1152]{3,2,0,1:T(8,128)(2,1)}, bf16[1,16,16,1152]{3,2,0,1:T(8,128)(2,1)S(1)}, u32[]{:S(2)}) copy-start(bf16[1,16,16,1152]{3,2,0,1:T(8,128)(2,1)S(1)} %fusion.16) | copy-start | bytes 1769476
  36.4 2.5 copy-start.9
  45.3 0.7 copy-start.16
  67.9 5.3 %copy-start.6 = (bf16[16,16,16,72]{3,2,1,0:T(8,128)(2,1)S(1)}, bf16[16,16,16,72]{3,2,1,0:T(8,128)(2,1)}, u32[]{:S(2)}) copy-start(bf16[16,16,16,72]{3,2,1,0:T(8,128)(2,1)} %convert_element_type.78) | copy-start | bytes 1769476
  73.2 1.3 copy-start.14
  73.2 1.4 copy-start.18
  87.0 254.5 %reduce-scatter.11.cloned.1.call-start = ((), (), s32[]{:S(2)}) async-start(), calls=%async_computation.4 | async-start | bytes 16920576
  93.3 1.0 copy-start.7
  99.4 4.7 copy-start.3
  99.4 4.7 copy-start.19
  104.0 9.0 %copy-start.17 = (f32[16,16,16]{2,1,0:T(8,128)S(1)}, f32[16,16,16]{2,1,0:T(8,128)}, u32[]{:S(2)}) copy-start(f32[16,16,16]{2,1,0:T(8,128)} %copy-done.16) | copy-start | bytes 49156
  104.0 9.2 %copy-start.15 = (f32[16,16,16]{0,2,1:T(8,128)S(1)}, f32[16,16,16]{0,2,1:T(8,128)}, u32[]{:S(2)}) copy-start(f32[16,16,16]{0,2,1:T(8,128)} %copy.90) | copy-start | bytes 49156
  116.4 4.4 copy-start.2
  116.5 4.4 copy-start.20
  135.7 2.4 copy-start.13
  135.7 2.5 copy-start.11
  138.1 7.9 %copy-start.8 = (bf16[256,3456]{1,0:T(8,128)(2,1)}, bf16[256,3456]{1,0:T(8,128)(2,1)S(1)}, u32[]{:S(2)}) copy-start(bf16[256,3456]{1,0:T(8,128)(2,1)S(1)} %constant_dynamic-update-slice_fusion) | copy-start | bytes 5308420
  152.6 1.0 copy-start.5
  154.0 187.6 %copy-start.21 = (u32[256]{0:T(256)S(1)}, u32[256]{0:T(256)}, u32[]{:S(2)}) copy-start(u32[256]{0:T(256)} %constant.32) | copy-start | bytes 3076
  154.0 369.1 %copy-start.1 = (bf16[1152,1152]{1,0:T(8,128)(2,1)S(1)}, bf16[1152,1152]{1,0:T(8,128)(2,1)}, u32[]{:S(2)}) copy-start(bf16[1152,1152]{1,0:T(8,128)(2,1)} %param.7) | copy-start | bytes 7962628
  156.6 186.8 %copy-start.12 = (bf16[1,1,256,1152]{3,2,1,0:T(8,128)(2,1)S(1)}, bf16[1,1,256,1152]{3,2,1,0:T(8,128)(2,1)}, u32[]{:S(2)}) copy-start(bf16[1,1,256,1152]{3,2,1,0:T(8,128)(2,1)} %param.5) | copy-start | bytes 1769476
  156.6 186.8 %all-to-all-start.1 = ((bf16[1,16,16,1152]{3,2,0,1:T(8,128)(2,1)}), bf16[1,16,16,1152]{3,2,0,1:T(8,128)(2,1)}, u32[]{:S(2)}, u32[]{:S(2)}) async-start(bf16[1,16,16,1152]{3,2,0,1:T(8,128)(2,1)} %fusion.28), calls=%async_computation.1 | async-start | bytes 1179648 | tf_op jit(solution)/shard_map/all_to_all | solution.py:94
  166.3 353.6 %all-reduce.7.cloned.1.call-start = ((), (), s32[]{:S(2)}) async-start(), calls=%async_computation.6 | async-start | bytes 2654208
Sparse Core Ops, SparseCore 0:
  87.1 73.2 reduce-scatter.12
  163.0 178.5 reduce-scatter.10
  344.5 175.3 all-reduce.6
where the time goes:
time: 538 us; the launch traced here: 530 us
  waiting for transfers between devices  350 us (65%)
  local copies, waits for them, and re-layouts  61.4 us (11%)
  matrix products  59.7 us (11%)
  other arithmetic  23.4 us (4%)
  starting transfers between devices  19.9 us (4%)
  between operations  15.7 us (3%)
    unnamed x6, waiting for transfers between devices  350 us
    dot_general x6, matrix products, batched(): return jnp.einsum(form, left, right, preferred_element_type=jnp.float32)  31.4 us
    unnamed x53, local copies, waits for them, and re-layouts  19.4 us
  transfers between devices with their start and end apart: 5, of which 2 were waited for; matrix products, arithmetic and copies ran while one was open for 22% of the time, Pallas kernels for 0%

commit v1 on v0

v1 whole, which is shorter than its diff:
```python
import functools

import jax
import jax.numpy as jnp
from jax import lax
from jax.experimental import pallas as pl
from jax.experimental.pallas import tpu as pltpu
from jax.sharding import PartitionSpec as P

F32, BF16 = jnp.float32, jnp.bfloat16
EPS = 1e-06
HEADS = 16
HD = 72
D = 1152
FR = 16
PX = 16
TOK = FR * PX
FACTOR = HD**-0.5
NT = (((1,), (1,)), ((), ()))
TN = (((0,), (0,)), ((), ()))
ROWS_A, ROWS_B = 80, 64
MIB = 1 << 20


def dot(a, b, dims=None):
    if dims is None:
        return jnp.dot(a, b, preferred_element_type=F32)
    return lax.dot_general(a, b, dims, preferred_element_type=F32)


def seq_peer(offset):
    return {"seq": lax.rem(lax.axis_index("seq") + offset, 16)}


def place():
    dp, seq = lax.axis_index("dp"), lax.axis_index("seq")
    return dp // 4, (dp // 2) % 2, dp % 2, seq // 4, seq % 4


def spread_kernel(dout_ref, up_ref, send_sems, recv_sems, own_sem):
    me = lax.axis_index("seq")
    barrier = pltpu.get_barrier_semaphore()
    for o in range(1, 16):
        pl.semaphore_signal(barrier, inc=1, device_id=seq_peer(o))
    pl.semaphore_wait(barrier, 15)

    def piece(o):
        return pltpu.make_async_remote_copy(
            src_ref=dout_ref.at[lax.rem(me + o, 16)],
            dst_ref=up_ref.at[me],
            send_sem=send_sems.at[o],
            recv_sem=recv_sems.at[o],
            device_id=seq_peer(o),
        )

    own = pltpu.make_async_copy(dout_ref.at[me], up_ref.at[me], own_sem)
    own.start()
    for o in range(1, 16):
        piece(o).start()
    own.wait()
    for o in range(1, 16):
        piece(o).wait()


def spread(dout):
    return pl.pallas_call(
        spread_kernel,
        out_shape=jax.ShapeDtypeStruct((16, PX, D), BF16),
        in_specs=[pl.BlockSpec(memory_space=pltpu.VMEM)],
        out_specs=pl.BlockSpec(memory_space=pltpu.VMEM),
        scratch_shapes=[
            pltpu.SemaphoreType.DMA((16,)),
            pltpu.SemaphoreType.DMA((16,)),
            pltpu.SemaphoreType.DMA,
        ],
        compiler_params=pltpu.CompilerParams(collective_id=1, has_side_effects=True),
    )(dout)


def to_rows(block):
    return jnp.concatenate([block[:, 8 * p : 8 * p + 8, :].reshape(128, D) for p in range(2)], axis=0)


def from_rows(rows):
    return jnp.concatenate([rows[128 * p : 128 * p + 128].reshape(FR, 8, D) for p in range(2)], axis=1)


def attend(q, k, v, ga, mask):
    rq = lax.rsqrt(jnp.sum(q * q, axis=0, keepdims=True) * (1.0 / HD) + EPS)
    rk = lax.rsqrt(jnp.sum(k * k, axis=0, keepdims=True) * (1.0 / HD) + EPS)
    qn, kn = (q * rq).astype(BF16), (k * rk).astype(BF16)
    vb, gb = v.astype(BF16), ga.astype(BF16)
    out = []
    for p in range(2):
        at = slice(128 * p, 128 * p + 128)
        qh, kh, vh, gh = qn[:, at], kn[:, at], vb[:, at], gb[:, at]
        e = jnp.exp(dot(kh, qh, TN) * FACTOR).reshape(FR, 8, 128)
        probs = e * (mask / jnp.sum(e, axis=0))[None]
        pb = probs.reshape(128, 128).astype(BF16)
        att = dot(vh, pb)
        grad_probs = dot(vh, gh, TN).reshape(FR, 8, 128)
        total = jnp.sum(probs * grad_probs, axis=0)
        gs = (probs * (grad_probs - total[None]) * FACTOR).reshape(128, 128).astype(BF16)
        gv = dot(gh, pb, NT)
        gqn = dot(kh, gs)
        gkn = dot(qh, gs, NT)
        out.append((att, gqn, gkn, gv))
    att, gqn, gkn, gv = (jnp.concatenate(pair, axis=1) for pair in zip(*out))
    tq = jnp.sum(gqn * q, axis=0, keepdims=True) * (1.0 / HD)
    tk = jnp.sum(gkn * k, axis=0, keepdims=True) * (1.0 / HD)
    gq = rq * gqn - q * (rq * rq * rq * tq)
    gk = rk * gkn - k * (rk * rk * rk * tk)
    return att, gq, gk, gv


def local_kernel(x_ref, up_ref, wqkv_ref, wout_ref, branch_ref, nt_ref, at_ref, gp_ref, ut_ref, std, proj, gat):
    x = to_rows(x_ref[...].astype(F32))
    centred = x - jnp.mean(x, axis=-1, keepdims=True)
    inverse = lax.rsqrt(jnp.mean(centred * centred, axis=-1, keepdims=True) + EPS)
    standard = centred * inverse
    std[...] = standard
    normed = standard.astype(BF16)
    standard_t = standard.T
    for c in range(2):
        nt_ref[c] = jnp.concatenate(
            [standard_t[HD * (2 * b + c) : HD * (2 * b + c + 1)] for b in range(8)], axis=0
        ).astype(BF16)
    for t in range(3):
        proj[D * t : D * t + D, :] = dot(normed, wqkv_ref[:, D * t : D * t + D]).T
    ut = to_rows(up_ref[...].astype(F32)).T.astype(BF16)
    ut_ref[0:96, :] = jnp.zeros((96, TOK), BF16)
    ut_ref[96 : 96 + D, :] = ut
    gat[...] = dot(wout_ref[...], ut)
    gp_ref[3 * D : 3 * D + 32, :] = jnp.zeros((32, TOK), BF16)
    mask = (
        lax.broadcasted_iota(jnp.int32, (8, 128), 0) == lax.broadcasted_iota(jnp.int32, (8, 128), 1) % 8
    ).astype(F32)

    def group(i, carry):
        base = pl.multiple_of(i * 288, 288)
        blocks = [proj[pl.ds(pl.multiple_of(D * t + base, 288), 288), :] for t in range(3)]
        blocks.append(gat[pl.ds(base, 288), :])
        heads = [attend(*(b[HD * h : HD * h + HD] for b in blocks), mask) for h in range(4)]
        half = pl.multiple_of(i * 144, 144)
        for c in range(2):
            at_ref[c, pl.ds(half, 144), :] = jnp.concatenate([heads[c][0], heads[c + 2][0]], axis=0).astype(BF16)
        for t in range(3):
            gp_ref[pl.ds(pl.multiple_of(D * t + base, 288), 288), :] = jnp.concatenate(
                [h[1 + t] for h in heads], axis=0
            ).astype(BF16)
        return carry

    lax.fori_loop(0, 4, group, 0)
    gn = dot(wqkv_ref[...], gp_ref[0 : 3 * D, :]).T
    standard = std[...]
    branch = inverse * (
        gn
        - jnp.mean(gn, axis=-1, keepdims=True)
        - standard * jnp.mean(gn * standard, axis=-1, keepdims=True)
    )
    branch_ref[...] = from_rows(branch).astype(BF16)


def local_math(x, up, wqkv, wout):
    vmem = pl.BlockSpec(memory_space=pltpu.VMEM)
    return pl.pallas_call(
        local_kernel,
        out_shape=[
            jax.ShapeDtypeStruct((FR, PX, D), BF16),
            jax.ShapeDtypeStruct((2, D // 2, TOK), BF16),
            jax.ShapeDtypeStruct((2, D // 2, TOK), BF16),
            jax.ShapeDtypeStruct((3 * D + 32, TOK), BF16),
            jax.ShapeDtypeStruct((D + 96, TOK), BF16),
        ],
        in_specs=[vmem] * 4,
        out_specs=[vmem] * 5,
        scratch_shapes=[
            pltpu.VMEM((TOK, D), F32),
            pltpu.VMEM((3 * D, TOK), F32),
            pltpu.VMEM((D, TOK), F32),
        ],
        compiler_params=pltpu.CompilerParams(vmem_limit_bytes=48 * MIB),
    )(x, up, wqkv, wout)


def reduce_kernel(
    nt, at, gp, ut, branch, dout, d_x1, g_qkv, g_out,
    pn, pa, pg, pu, s1, s2, r1, r2, t1, t2, u1, u2, total, zs, zr, kept, hs, hr, back,
    pair_s, pair_r, back_s, back_r, x_s, x_r, y_s, y_r, x2_s, x2_r, y2_s, y2_r, zl_s, zl_r, zh_s, zh_r,
):
    dp, seq = lax.axis_index("dp"), lax.axis_index("seq")
    y, zl, core, x, zh = place()

    def x_peer(o):
        return {"seq": lax.rem(x + o, 4) * 4 + zh}

    def zh_peer(o):
        return {"seq": x * 4 + lax.rem(zh + o, 4)}

    def y_peer(o):
        return {"dp": lax.rem(y + o, 4) * 4 + zl * 2 + core}

    core_peer = {"dp": dp + 1 - 2 * core}
    zl_peer = {"dp": dp + 2 - 4 * zl}
    barrier = pltpu.get_barrier_semaphore()
    for peer in [seq_peer(o) for o in range(1, 16)] + [y_peer(o) for o in range(1, 4)] + [core_peer, zl_peer]:
        pl.semaphore_signal(barrier, inc=1, device_id=peer)
    pl.semaphore_wait(barrier, 20)

    def send(src, dst, s_sem, r_sem, peer):
        copy = pltpu.make_async_remote_copy(src_ref=src, dst_ref=dst, send_sem=s_sem, recv_sem=r_sem, device_id=peer)
        return copy

    pair = [
        send(nt.at[1 - core], pn, pair_s.at[0], pair_r.at[0], core_peer),
        send(gp, pg, pair_s.at[1], pair_r.at[1], core_peer),
        send(at.at[1 - core], pa, pair_s.at[2], pair_r.at[2], core_peer),
        send(ut, pu, pair_s.at[3], pair_r.at[3], core_peer),
    ]
    for copy in pair:
        copy.start()
    returns = [
        send(branch.at[lax.rem(seq + o, 16)], back.at[seq], back_s.at[o], back_r.at[o], seq_peer(o))
        for o in range(1, 16)
    ]
    for copy in returns:
        copy.start()
    for copy in pair:
        copy.wait()

    lane = lax.broadcasted_iota(jnp.int32, (D // 2, 128), 1)
    first, second = [], []
    for step, o in enumerate((2, 1, 3, 0)):
        xd = lax.rem(x + o, 4)
        q_rows = pl.ds(pl.multiple_of(xd * 864, 16), 896)
        o_rows = pl.ds(pl.multiple_of(xd * 288, 16), 384)
        left = dot(nt[core], gp[q_rows, :], NT) + dot(pn[...], pg[q_rows, :], NT)
        right = dot(at[core], ut[o_rows, :], NT) + dot(pa[...], pu[o_rows, :], NT)
        middle = jnp.where(lane < 96, left[:, 768:896], right[:, 0:128])
        for cols, val in ((slice(0, 768), left[:, 0:768]), (slice(768, 896), middle), (slice(896, D), right[:, 128:384])):
            val = val.astype(BF16)
            for b in range(4):
                s1[xd, b, :, cols] = val[144 * b : 144 * b + ROWS_A]
                s2[b, xd, :, cols] = val[144 * b + ROWS_A : 144 * b + 144]
        if o:
            copy = send(s1.at[xd], r1.at[o - 1], x_s.at[o - 1], x_r.at[o - 1], x_peer(o))
            copy.start()
            first.append(copy)
        for oy in (2, 1, 3):
            yd = lax.rem(y + oy, 4)
            copy = send(
                s2.at[yd, xd], r2.at[oy - 1, xd], y_s.at[step * 3 + oy - 1], y_r.at[step * 3 + oy - 1], y_peer(oy)
            )
            copy.start()
            second.append(copy)

    for copy in first:
        copy.wait()
    for copy in second:
        copy.wait()

    def add(own, *others):
        value = own.astype(F32)
        for other in others:
            value = value + other.astype(F32)
        return value

    later = []
    for o in (2, 1, 3, 0):
        yd, xd = lax.rem(y + o, 4), lax.rem(x + o, 4)
        t1[yd] = add(s1[x, yd], r1[0, yd], r1[1, yd], r1[2, yd]).astype(BF16)
        t2[xd] = add(s2[y, xd], r2[0, xd], r2[1, xd], r2[2, xd]).astype(BF16)
        if o:
            later.append(send(t1.at[yd], u1.at[o - 1], y2_s.at[o - 1], y2_r.at[o - 1], y_peer(o)))
            later[-1].start()
            later.append(send(t2.at[xd], u2.at[o - 1], x2_s.at[o - 1], x2_r.at[o - 1], x_peer(o)))
            later[-1].start()
    for copy in later:
        copy.wait()
    total[0:ROWS_A, :] = add(t1[y], u1[0], u1[1], u1[2])
    total[ROWS_A:144, :] = add(t2[x], u2[0], u2[1], u2[2])

    zs[...] = total[pl.ds(pl.multiple_of(64 * (1 - zl), 64), 80), :].astype(BF16)
    copy = send(zs, zr, zl_s, zl_r, zl_peer)
    copy.start()
    for copy_back in returns:
        copy_back.wait()
    back[seq] = branch[seq]
    d_x1[...] = (dout[...].astype(F32) + back[...].astype(F32)).astype(BF16)
    copy.wait()
    kept[...] = total[pl.ds(pl.multiple_of(64 * zl, 64), 80), :] + zr[...].astype(F32)
    value = kept[pl.ds(pl.multiple_of(8 * zl, 8), 72), :]
    hs[...] = jnp.zeros_like(hs)
    for b in range(4):
        hs[b, 0:72, 0:216] = value[:, 216 * b : 216 * b + 216].astype(BF16)
        hs[b, 0:72, 256:328] = value[:, 864 + 72 * b : 936 + 72 * b].astype(BF16)
    ends = [
        send(hs.at[lax.rem(zh + o, 4)], hr.at[o - 1], zh_s.at[o - 1], zh_r.at[o - 1], zh_peer(o)) for o in (2, 1, 3)
    ]
    for copy in ends:
        copy.start()
    for copy in ends:
        copy.wait()
    result = add(hs[zh], hr[0], hr[1], hr[2]) * (1.0 / 256.0)
    g_qkv[...] = result[0:72, 0:216]
    g_out[...] = result[0:72, 256:328]


def reduce_all(nt, at, gp, ut, branch, dout):
    vmem = pl.BlockSpec(memory_space=pltpu.VMEM)
    half = D // 2
    dma = pltpu.SemaphoreType.DMA
    return pl.pallas_call(
        reduce_kernel,
        out_shape=[
            jax.ShapeDtypeStruct((16, PX, D), BF16),
            jax.ShapeDtypeStruct((72, 216), F32),
            jax.ShapeDtypeStruct((72, 72), F32),
        ],
        in_specs=[vmem] * 6,
        out_specs=[vmem] * 3,
        scratch_shapes=[
            pltpu.VMEM((half, TOK), BF16),
            pltpu.VMEM((half, TOK), BF16),
            pltpu.VMEM((3 * D + 32, TOK), BF16),
            pltpu.VMEM((D + 96, TOK), BF16),
            pltpu.VMEM((4, 4, ROWS_A, D), BF16),
            pltpu.VMEM((4, 4, ROWS_B, D), BF16),
            pltpu.VMEM((3, 4, ROWS_A, D), BF16),
            pltpu.VMEM((3, 4, ROWS_B, D), BF16),
            pltpu.VMEM((4, ROWS_A, D), BF16),
            pltpu.VMEM((4, ROWS_B, D), BF16),
            pltpu.VMEM((3, ROWS_A, D), BF16),
            pltpu.VMEM((3, ROWS_B, D), BF16),
            pltpu.VMEM((144, D), F32),
            pltpu.VMEM((80, D), BF16),
            pltpu.VMEM((80, D), BF16),
            pltpu.VMEM((80, D), F32),
            pltpu.VMEM((4, 80, 384), BF16),
            pltpu.VMEM((3, 80, 384), BF16),
            pltpu.VMEM((16, PX, D), BF16),
            dma((4,)), dma((4,)),
            dma((16,)), dma((16,)),
            dma((3,)), dma((3,)),
            dma((12,)), dma((12,)),
            dma((3,)), dma((3,)),
            dma((3,)), dma((3,)),
            dma, dma,
            dma((3,)), dma((3,)),
        ],
        compiler_params=pltpu.CompilerParams(
            collective_id=2, has_side_effects=True, vmem_limit_bytes=48 * MIB
        ),
    )(nt, at, gp, ut, branch, dout)


def local(x1_pixels, dout_frames, w_qkv, w_out):
    x = x1_pixels.reshape(FR, PX, D)
    dout = dout_frames.reshape(16, PX, D)
    up = spread(dout)
    branch, nt, at, gp, ut = local_math(x, up, w_qkv, w_out)
    d_x1, g_qkv, g_out = reduce_all(nt, at, gp, ut, branch, dout)
    return d_x1.reshape(dout_frames.shape), g_qkv, g_out


def solution(mesh):
    return jax.shard_map(
        local,
        mesh=mesh,
        in_specs=(P("dp", None, "seq", None), P("dp", "seq", None, None), P(), P()),
        out_specs=(P("dp", "seq", None, None), P("dp", "seq"), P("dp", "seq")),
        check_vma=False,
    )
```

time: 538 us -> 126 us (0.23); the launches traced: 530 us -> 126 us
  waiting for transfers between devices: 350 us -> 0 us
  Pallas kernels: 0 us -> 121 us
  matrix products: 59.7 us -> 0 us
  local copies, waits for them, and re-layouts: 61.4 us -> 4.19 us
  other arithmetic: 23.4 us -> 0 us
  starting transfers between devices: 19.9 us -> 0 us
  between operations: 15.7 us -> 0.67 us
    unnamed x6 -> x0, waiting for transfers between devices: 350 us -> none
    pallas_call x0 -> x3, Pallas kernels: none -> 121 us  [the longest x1 76.4 us: reduce_all(): pl.pallas_call(reduce_kernel, out_shape=[jax.ShapeDtypeStruct((16, PX, D)...]
    dot_general x11 -> x0, matrix products: 59.7 us -> none  [the longest x6 31.4 us: batched(): return jnp.einsum(form, left, right, preferred_element_type=jnp.float32)]
    reshape x8 -> x0, local copies, waits for them, and re-layouts: 25.8 us -> none  [the longest x2 8.04 us: temporal_terms(): query = projected[:, :width].reshape(split_shape)]
    all_to_all x2 -> x0, starting transfers between devices: 19.8 us -> none  [the longest x1 10.2 us: local(): lax.all_to_all(dout_frames, 'seq', split_axis=2, concat_axis=1, tiled=True)]
    unnamed x53 -> x9, local copies, waits for them, and re-layouts: 19.4 us -> 4.19 us
    another operation x2 -> x0, other arithmetic: 6.46 us -> none
    unnamed x1 -> x0, other arithmetic: 5.99 us -> none
  transfers between devices with their start and end apart: 5 -> 0, of which waited for: 2 -> 0; matrix products, arithmetic and copies ran while one was open for 22% -> 0% of each run, Pallas kernels for 0% -> 0%
where the time goes in v1:
time: 126 us
  Pallas kernels  121 us (96%)
  local copies, waits for them, and re-layouts  4.19 us (3%)
    pallas_call x1, Pallas kernels, reduce_all(): pl.pallas_call(reduce_kernel, out_shape=[jax.ShapeDtypeStruct((16, PX, D)...  76.4 us
    pallas_call x1, Pallas kernels, spread(): pl.pallas_call(spread_kernel, out_shape=jax.ShapeDtypeStruct((16, PX, D),...  25.2 us
    pallas_call x1, Pallas kernels, local_math(): pl.pallas_call(local_kernel, out_shape=[jax.ShapeDtypeStruct((FR, PX, D),...  19 us
    unnamed x9, local copies, waits for them, and re-layouts  4.19 us

profile of v1, /device:TPU:32, one launch (start us, length us, event | category | flops | bytes accessed | tf_op | source)
XLA Modules:
  0.0 125.6 jit_solution(15381845159451372668)
XLA Ops:
  0.6 25.2 %shard_map.67.up_ref = bf16[16,16,1152]{2,1,0:T(8,128)(2,1)} custom-call(bf16[16,16,1152]{2,1,0:T(8,128)(2,1)} %bitcast.3), custom_call_target="tpu_custom_call" | custom-call | tf_op jit(solution)/shard_map/pallas_call | solution.py:66
  25.9 0.0 copy-start.1
  25.9 1.1 copy-done.1
  26.9 0.0 copy-start.2
  26.9 1.1 copy-done.2
  28.0 0.0 copy-start
  28.0 19.0 %shard_map.68 = (bf16[16,16,1152]{2,1,0:T(8,128)(2,1)S(1)}, bf16[2,576,256]{2,1,0:T(8,128)(2,1)S(1)}, bf16[2,576,256]{2,1,0:T(8,128)(2,1)S(1)}, bf16[3488,256]{1,0:T(8,128)(2,1)S(1)}, bf16[1248,256]{1,0:T(8,128)(2,1)S(1)}) custom-call(bf16[16,16,1152]{2,1,0:T(8,128)(2,1)S(1)} %bitcast.5, bf16[16,16,1152]{2,1,0:T(8,128)(2,1)S(1)} %copy-done.1, ...), custom_call_target="tpu_custom_call" | custom-call | tf_op jit(solution)/shard_map/pallas_call | solution.py:166
  47.0 0.0 copy-done
  47.0 76.4 %shard_map.69 = (bf16[16,16,1152]{2,1,0:T(8,128)(2,1)S(1)}, f32[72,216]{1,0:T(8,128)S(1)}, f32[72,72]{1,0:T(8,128)S(1)}) custom-call(bf16[2,576,256]{2,1,0:T(8,128)(2,1)S(1)} %get-tuple-element.11.nt, bf16[2,576,256]{2,1,0:T(8,128)(2,1)S(1)} %get-tuple-element.12.at, bf16[3488,256]{1,0:T(8,128)(2,1)S(1)} %get-tuple-element.13.gp, ...), custom_call_target="tpu_custom_call" | custom-call | tf_op jit(solution)/shard_map/pallas_call | solution.py:313
  123.5 0.8 copy.10
  124.3 0.6 copy.11
  124.9 0.6 copy.12
Async XLA Ops:
  25.9 1.1 copy-start.1
  26.9 1.1 copy-start.2
  28.0 19.1 %copy-start = (bf16[1,1,256,1152]{3,2,1,0:T(8,128)(2,1)S(1)}, bf16[1,1,256,1152]{3,2,1,0:T(8,128)(2,1)}, u32[]{:S(2)}) copy-start(bf16[1,1,256,1152]{3,2,1,0:T(8,128)(2,1)} %param.5) | copy-start | bytes 1769476

commit v2 on v0

v2 whole, which is shorter than its diff:
```python
import jax
import jax.numpy as jnp
from jax import lax
from jax.experimental import pallas as pl
from jax.experimental.pallas import tpu as pltpu
from jax.sharding import PartitionSpec as P

F32, BF16 = jnp.float32, jnp.bfloat16
EPS = 1e-06
HD = 72
D = 1152
HALF = D // 2
FR = 16
PX = 16
TOK = FR * PX
FACTOR = HD**-0.5
NT = (((1,), (1,)), ((), ()))
TN = (((0,), (0,)), ((), ()))
ROWS_A, ROWS_B = 64, 80
QW, OW = 896, 384
MIB = 1 << 20


def dot(a, b, dims=None):
    if dims is None:
        return jnp.dot(a, b, preferred_element_type=F32)
    return lax.dot_general(a, b, dims, preferred_element_type=F32)


def to_rows(block):
    return jnp.concatenate([block[:, 8 * p : 8 * p + 8, :].reshape(128, D) for p in range(2)], axis=0)


def from_rows(rows):
    return jnp.concatenate([rows[128 * p : 128 * p + 128].reshape(FR, 8, D) for p in range(2)], axis=1)


def head_scale(v):
    return lax.rsqrt(jnp.sum(v * v, axis=0, keepdims=True) * (1.0 / HD) + EPS)


def forward_head(q, k, v, mask, keep):
    qn, kn, vb = (q * head_scale(q)).astype(BF16), (k * head_scale(k)).astype(BF16), v.astype(BF16)
    out = []
    for p in range(2):
        at = slice(128 * p, 128 * p + 128)
        e = jnp.exp(dot(kn[:, at], qn[:, at], TN) * FACTOR).reshape(FR, 8, 128)
        probs = (e * (mask / jnp.sum(e, axis=0))[None]).reshape(128, 128)
        keep(p, probs)
        out.append(dot(vb[:, at], probs.astype(BF16)))
    return jnp.concatenate(out, axis=1)


def backward_head(q, k, v, ga, probs_of):
    rq, rk = head_scale(q), head_scale(k)
    qn, kn = (q * rq).astype(BF16), (k * rk).astype(BF16)
    vb, gb = v.astype(BF16), ga.astype(BF16)
    out = []
    for p in range(2):
        at = slice(128 * p, 128 * p + 128)
        qh, kh, vh, gh = qn[:, at], kn[:, at], vb[:, at], gb[:, at]
        flat = probs_of(p)
        probs = flat.reshape(FR, 8, 128)
        pb = flat.astype(BF16)
        grad_probs = dot(vh, gh, TN).reshape(FR, 8, 128)
        total = jnp.sum(probs * grad_probs, axis=0)
        gs = (probs * (grad_probs - total[None]) * FACTOR).reshape(128, 128).astype(BF16)
        out.append((dot(kh, gs), dot(qh, gs, NT), dot(gh, pb, NT)))
    gqn, gkn, gv = (jnp.concatenate(pair, axis=1) for pair in zip(*out))
    tq = jnp.sum(gqn * q, axis=0, keepdims=True) * (1.0 / HD)
    tk = jnp.sum(gkn * k, axis=0, keepdims=True) * (1.0 / HD)
    gq = rq * gqn - q * (rq * rq * rq * tq)
    gk = rk * gkn - k * (rk * rk * rk * tk)
    return gq, gk, gv


def add(own, *others):
    value = own.astype(F32)
    for other in others:
        value = value + other.astype(F32)
    return value


def kernel(
    x_hbm, dout_hbm, wqkv_hbm, wout_hbm, back_ref, res_ref,
    xv, wqkv, wout, up, std, proj, gat, probs, branch, nt, at, gp, ut, pn, pa, pg, pu,
    s1, s2, so, r1, r2, ro, t1, t2, to, u1, u2, uo, total, zs, zr, kept, hs, hr,
    load, sp_s, sp_r, pair_s, pair_r, bk_s, bk_r, x_s, x_r, y_s, y_r, o_s, o_r,
    x2_s, x2_r, y2_s, y2_r, zl_s, zl_r, zh_s, zh_r,
):
    dp, seq = lax.axis_index("dp"), lax.axis_index("seq")
    y, zl, core, x, zh = dp // 4, (dp // 2) % 2, dp % 2, seq // 4, seq % 4

    def seq_peer(o):
        return {"seq": lax.rem(seq + o, 16)}

    def x_peer(o):
        return {"seq": lax.rem(x + o, 4) * 4 + zh}

    def zh_peer(o):
        return {"seq": x * 4 + lax.rem(zh + o, 4)}

    def y_peer(o):
        return {"dp": lax.rem(y + o, 4) * 4 + zl * 2 + core}

    core_peer = {"dp": dp + 1 - 2 * core}
    zl_peer = {"dp": dp + 2 - 4 * zl}

    def send(src, dst, s_sem, r_sem, peer):
        copy = pltpu.make_async_remote_copy(src_ref=src, dst_ref=dst, send_sem=s_sem, recv_sem=r_sem, device_id=peer)
        copy.start()
        return copy

    def wait(copies):
        for copy in copies:
            copy.wait()

    barrier = pltpu.get_barrier_semaphore()
    for peer in [seq_peer(o) for o in range(1, 16)] + [y_peer(o) for o in range(1, 4)] + [core_peer, zl_peer]:
        pl.semaphore_signal(barrier, inc=1, device_id=peer)
    loads = [
        pltpu.make_async_copy(x_hbm, xv, load.at[0]),
        pltpu.make_async_copy(wqkv_hbm, wqkv, load.at[1]),
        pltpu.make_async_copy(wout_hbm, wout, load.at[2]),
        pltpu.make_async_copy(dout_hbm.at[seq], up.at[seq], load.at[3]),
    ]
    for copy in loads:
        copy.start()
    pl.semaphore_wait(barrier, 20)
    order = (8, 7, 9, 6, 10, 5, 11, 4, 12, 3, 13, 2, 14, 1, 15)
    spread = [
        send(dout_hbm.at[lax.rem(seq + o, 16)], up.at[seq], sp_s.at[o], sp_r.at[o], seq_peer(o)) for o in order
    ]

    loads[0].wait()
    rows = to_rows(xv[...].astype(F32))
    centred = rows - jnp.mean(rows, axis=-1, keepdims=True)
    inverse = lax.rsqrt(jnp.mean(centred * centred, axis=-1, keepdims=True) + EPS)
    standard = centred * inverse
    std[...] = standard
    normed = standard.astype(BF16)
    standard_t = standard.T
    for c in range(2):
        nt[c] = jnp.concatenate(
            [standard_t[HD * (2 * b + c) : HD * (2 * b + c + 1)] for b in range(8)], axis=0
        ).astype(BF16)
    pair_n = send(nt.at[1 - core], pn, pair_s.at[12], pair_r.at[12], core_peer)
    loads[1].wait()
    for t in range(3):
        proj[D * t : D * t + D, :] = dot(normed, wqkv[:, D * t : D * t + D]).T

    mask = (
        lax.broadcasted_iota(jnp.int32, (8, 128), 0) == lax.broadcasted_iota(jnp.int32, (8, 128), 1) % 8
    ).astype(F32)

    def forward_group(i, carry):
        base = pl.multiple_of(i * 288, 288)
        blocks = [proj[pl.ds(pl.multiple_of(D * t + base, 288), 288), :] for t in range(3)]
        heads = []
        for h in range(4):

            def keep(p, value, h=h):
                probs[i * 4 + h, p] = value

            heads.append(forward_head(*(b[HD * h : HD * h + HD] for b in blocks), mask, keep))
        half = pl.multiple_of(i * 144, 144)
        for c in range(2):
            at[c, pl.ds(half, 144), :] = jnp.concatenate([heads[c], heads[c + 2]], axis=0).astype(BF16)
        return carry

    lax.fori_loop(0, 4, forward_group, 0)
    pair_a = send(at.at[1 - core], pa, pair_s.at[13], pair_r.at[13], core_peer)

    loads[2].wait()
    loads[3].wait()
    wait(spread)
    up_t = to_rows(up[...].astype(F32)).T.astype(BF16)
    ut[...] = up_t
    pair_u = send(ut, pu, pair_s.at[14], pair_r.at[14], core_peer)
    gat[...] = dot(wout[...], up_t)
    wait([pair_n, pair_a, pair_u])

    own_a = at[core]
    for n in range(3):
        cols = slice(OW * n, OW * n + OW)
        val = (dot(own_a, ut[cols, :], NT) + dot(pa[...], pu[cols, :], NT)).astype(BF16)
        for b in range(4):
            so[b, :, cols] = val[144 * b : 144 * b + 144]
    out_y = []
    for o in (2, 1, 3):
        out_y.append(send(so.at[lax.rem(y + o, 4)], ro.at[o - 1], o_s.at[o - 1], o_r.at[o - 1], y_peer(o)))

    gp[3 * D : 3 * D + 32, :] = jnp.zeros((32, TOK), BF16)
    pg[3 * D : 3 * D + 32, :] = jnp.zeros((32, TOK), BF16)

    def gp_copy(i, t):
        span = pl.ds(pl.multiple_of(D * t + i * 288, 288), 288)
        return pltpu.make_async_remote_copy(
            src_ref=gp.at[span], dst_ref=pg.at[span],
            send_sem=pair_s.at[3 * i + t], recv_sem=pair_r.at[3 * i + t], device_id=core_peer,
        )

    def backward_group(i, carry):
        base = pl.multiple_of(i * 288, 288)
        blocks = [proj[pl.ds(pl.multiple_of(D * t + base, 288), 288), :] for t in range(3)]
        blocks.append(gat[pl.ds(base, 288), :])
        heads = [
            backward_head(*(b[HD * h : HD * h + HD] for b in blocks), lambda p, h=h: probs[i * 4 + h, p])
            for h in range(4)
        ]
        for t in range(3):
            gp[pl.ds(pl.multiple_of(D * t + base, 288), 288), :] = jnp.concatenate(
                [h[t] for h in heads], axis=0
            ).astype(BF16)
            gp_copy(i, t).start()
        return carry

    lax.fori_loop(0, 4, backward_group, 0)
    wait([gp_copy(i, t) for i in range(4) for t in range(3)])

    own_n = nt[core]
    first, second = [], []
    for step, o in enumerate((2, 1, 3, 0)):
        xd = lax.rem(x + o, 4)
        span = pl.ds(pl.multiple_of(xd * 864, 16), QW)
        val = (dot(own_n, gp[span, :], NT) + dot(pn[...], pg[span, :], NT)).astype(BF16)
        for b in range(4):
            s1[xd, b] = val[144 * b : 144 * b + ROWS_A]
            s2[b, xd] = val[144 * b + ROWS_A : 144 * b + 144]
        if o:
            first.append(send(s1.at[xd], r1.at[o - 1], x_s.at[o - 1], x_r.at[o - 1], x_peer(o)))
        for oy in (2, 1, 3):
            sem = step * 3 + oy - 1
            second.append(
                send(s2.at[lax.rem(y + oy, 4), xd], r2.at[oy - 1, xd], y_s.at[sem], y_r.at[sem], y_peer(oy))
            )

    gn = dot(wqkv[...], gp[0 : 3 * D, :]).T
    standard = std[...]
    value = inverse * (
        gn
        - jnp.mean(gn, axis=-1, keepdims=True)
        - standard * jnp.mean(gn * standard, axis=-1, keepdims=True)
    )
    branch[...] = from_rows(value).astype(BF16)
    returns = [
        send(branch.at[lax.rem(seq + o, 16)], back_ref.at[seq], bk_s.at[o], bk_r.at[o], seq_peer(o)) for o in order
    ]
    back_ref[seq] = branch[seq]

    wait(out_y)
    val = add(so[y], ro[0], ro[1], ro[2]).astype(BF16)
    for b in range(4):
        to[b, :, 0:288] = val[:, 288 * b : 288 * b + 288]
        to[b, :, 288:OW] = jnp.zeros((144, OW - 288), BF16)
    later = [
        send(to.at[lax.rem(x + o, 4)], uo.at[o - 1], x2_s.at[o + 2], x2_r.at[o + 2], x_peer(o)) for o in (2, 1, 3)
    ]
    wait(first)
    for o in (2, 1, 3, 0):
        yd = lax.rem(y + o, 4)
        t1[yd] = add(s1[x, yd], r1[0, yd], r1[1, yd], r1[2, yd]).astype(BF16)
        if o:
            later.append(send(t1.at[yd], u1.at[o - 1], y2_s.at[o - 1], y2_r.at[o - 1], y_peer(o)))
    wait(second)
    for o in (2, 1, 3, 0):
        xd = lax.rem(x + o, 4)
        t2[xd] = add(s2[y, xd], r2[0, xd], r2[1, xd], r2[2, xd]).astype(BF16)
        if o:
            later.append(send(t2.at[xd], u2.at[o - 1], x2_s.at[o - 1], x2_r.at[o - 1], x_peer(o)))
    wait(later)
    total[0:ROWS_A, 0:QW] = add(t1[y], u1[0], u1[1], u1[2])
    total[ROWS_A:144, 0:QW] = add(t2[x], u2[0], u2[1], u2[2])
    total[:, QW:] = add(to[x], uo[0], uo[1], uo[2])

    zs[...] = total[pl.ds(pl.multiple_of(64 * (1 - zl), 64), 80), :].astype(BF16)
    send(zs, zr, zl_s, zl_r, zl_peer).wait()
    kept[...] = total[pl.ds(pl.multiple_of(64 * zl, 64), 80), :] + zr[...].astype(F32)
    value = kept[pl.ds(pl.multiple_of(8 * zl, 8), 72), :]

    hs[...] = jnp.zeros_like(hs)
    for b in range(4):
        hs[b, 0:72, 0:216] = value[:, 216 * b : 216 * b + 216].astype(BF16)
        hs[b, 0:72, 256:328] = value[:, QW + 72 * b : QW + 72 * b + 72].astype(BF16)
    wait(
        [
            send(hs.at[lax.rem(zh + o, 4)], hr.at[o - 1], zh_s.at[o - 1], zh_r.at[o - 1], zh_peer(o))
            for o in (2, 1, 3)
        ]
    )
    res_ref[...] = add(hs[zh], hr[0], hr[1], hr[2])
    wait(returns)


def fused(x, dout, wqkv, wout):
    dma = pltpu.SemaphoreType.DMA

    def buf(*shape, dtype=BF16):
        return pltpu.VMEM(shape, dtype)

    return pl.pallas_call(
        kernel,
        out_shape=[jax.ShapeDtypeStruct((16, PX, D), BF16), jax.ShapeDtypeStruct((80, OW), F32)],
        in_specs=[pl.BlockSpec(memory_space=pl.ANY)] * 4,
        out_specs=[pl.BlockSpec(memory_space=pltpu.VMEM)] * 2,
        scratch_shapes=[
            buf(FR, PX, D), buf(D, 3 * D), buf(D, D), buf(16, PX, D),
            buf(TOK, D, dtype=F32), buf(3 * D, TOK, dtype=F32), buf(D, TOK, dtype=F32),
            buf(16, 2, 128, 128, dtype=F32), buf(FR, PX, D),
            buf(2, HALF, TOK), buf(2, HALF, TOK), buf(3 * D + 32, TOK), buf(D, TOK),
            buf(HALF, TOK), buf(HALF, TOK), buf(3 * D + 32, TOK), buf(D, TOK),
            buf(4, 4, ROWS_A, QW), buf(4, 4, ROWS_B, QW), buf(4, 144, D),
            buf(3, 4, ROWS_A, QW), buf(3, 4, ROWS_B, QW), buf(3, 144, D),
            buf(4, ROWS_A, QW), buf(4, ROWS_B, QW), buf(4, 144, OW),
            buf(3, ROWS_A, QW), buf(3, ROWS_B, QW), buf(3, 144, OW),
            buf(144, QW + OW, dtype=F32), buf(80, QW + OW), buf(80, QW + OW),
            buf(80, QW + OW, dtype=F32), buf(4, 80, OW), buf(3, 80, OW),
            dma((4,)), dma((16,)), dma((16,)), dma((15,)), dma((15,)), dma((16,)), dma((16,)),
            dma((3,)), dma((3,)), dma((12,)), dma((12,)), dma((3,)), dma((3,)),
            dma((6,)), dma((6,)), dma((3,)), dma((3,)), dma, dma, dma((3,)), dma((3,)),
        ],
        compiler_params=pltpu.CompilerParams(
            collective_id=1, has_side_effects=True, vmem_limit_bytes=56 * MIB
        ),
    )(x, dout, wqkv, wout)


def local(x1_pixels, dout_frames, w_qkv, w_out):
    x = x1_pixels.reshape(FR, PX, D)
    dout = dout_frames.reshape(16, PX, D)
    back, res = fused(x, dout, w_qkv, w_out)
    d_x1 = (dout.astype(F32) + back.astype(F32)).astype(BF16).reshape(dout_frames.shape)
    res = res * (1.0 / 256.0)
    return d_x1, res[0:72, 0:216], res[0:72, 256:328]


def solution(mesh):
    return jax.shard_map(
        local,
        mesh=mesh,
        in_specs=(P("dp", None, "seq", None), P("dp", "seq", None, None), P(), P()),
        out_specs=(P("dp", "seq", None, None), P("dp", "seq"), P("dp", "seq")),
        check_vma=False,
    )
```

time: 538 us -> 101 us (0.19); the launches traced: 530 us -> 101 us
  waiting for transfers between devices: 350 us -> 0 us
  Pallas kernels: 0 us -> 97.1 us
  local copies, waits for them, and re-layouts: 61.4 us -> 1.27 us
  matrix products: 59.7 us -> 0 us
  other arithmetic: 23.4 us -> 2.06 us
  starting transfers between devices: 19.9 us -> 0 us
  between operations: 15.7 us -> 0.67 us
    unnamed x6 -> x0, waiting for transfers between devices: 350 us -> none
    pallas_call x0 -> x1, Pallas kernels: none -> 97.1 us  [fused(): pl.pallas_call(kernel, out_shape=[jax.ShapeDtypeStruct((16, PX, D), BF16)...]
    dot_general x11 -> x0, matrix products: 59.7 us -> none  [the longest x6 31.4 us: batched(): return jnp.einsum(form, left, right, preferred_element_type=jnp.float32)]
    reshape x8 -> x0, local copies, waits for them, and re-layouts: 25.8 us -> none  [the longest x2 8.04 us: temporal_terms(): query = projected[:, :width].reshape(split_shape)]
    all_to_all x2 -> x0, starting transfers between devices: 19.8 us -> none  [the longest x1 10.2 us: local(): lax.all_to_all(dout_frames, 'seq', split_axis=2, concat_axis=1, tiled=True)]
    unnamed x53 -> x4, local copies, waits for them, and re-layouts: 19.4 us -> 0.01 us
    another operation x2 -> x0, other arithmetic: 6.46 us -> none
    unnamed x1 -> x0, other arithmetic: 5.99 us -> none
  transfers between devices with their start and end apart: 5 -> 0, of which waited for: 2 -> 0; matrix products, arithmetic and copies ran while one was open for 22% -> 0% of each run, Pallas kernels for 0% -> 0%
where the time goes in v2:
time: 101 us
  Pallas kernels  97.1 us (96%)
  other arithmetic  2.06 us (2%)
  local copies, waits for them, and re-layouts  1.27 us (1%)
    pallas_call x1, Pallas kernels, fused(): pl.pallas_call(kernel, out_shape=[jax.ShapeDtypeStruct((16, PX, D), BF16)...  97.1 us
    convert_element_type x1, other arithmetic, local(): (dout.astype(F32) + back.astype(F32)).astype(BF16)  2.05 us

profile of v2, /device:TPU:32, one launch (start us, length us, event | category | flops | bytes accessed | tf_op | source)
XLA Modules:
  0.0 101.1 jit_solution(10966985142949458253)
XLA Ops:
  0.6 0.0 copy-start
  0.6 97.1 %shard_map.67 = (bf16[16,16,1152]{2,1,0:T(8,128)(2,1)}, f32[80,384]{1,0:T(8,128)}) custom-call(bf16[16,16,1152]{2,1,0:T(8,128)(2,1)} %bitcast.5, bf16[16,16,1152]{2,1,0:T(8,128)(2,1)} %bitcast.3, bf16[1152,3456]{1,0:T(8,128)(2,1)} %wqkv_hbm.1, bf16[1152,1152]{1,0:T(8,128)(2,1)} %wout_hbm.1), custom_call_target="tpu_custom_call" | custom-call | tf_op jit(solution)/shard_map/pallas_call | solution.py:301
  97.8 0.0 copy-start.1
  97.8 0.0 copy-done
  97.8 2.1 %add_convert_fusion = bf16[16,16,1152]{2,1,0:T(8,128)(2,1)} fusion(bf16[16,16,1152]{2,1,0:T(8,128)(2,1)} %get-tuple-element.5, bf16[16,16,1152]{2,1,0:T(8,128)(2,1)S(1)} %bitcast.4), kind=kLoop, calls=%fused_computation | loop fusion | flops 1179648 | bytes 1769472 | tf_op jit(solution)/shard_map/convert_element_type | solution.py:332
  99.8 0.0 copy-done.1
  99.8 0.6 slice.9
  100.5 0.6 slice.8
  (1 shorter events, 0.0 us)
Async XLA Ops:
  0.6 97.1 %copy-start = (bf16[1,1,256,1152]{3,2,1,0:T(8,128)(2,1)S(1)}, bf16[1,1,256,1152]{3,2,1,0:T(8,128)(2,1)}, u32[]{:S(2)}) copy-start(bf16[1,1,256,1152]{3,2,1,0:T(8,128)(2,1)} %param.5) | copy-start | bytes 1769476
  97.8 2.1 %copy-start.1 = (f32[80,384]{1,0:T(8,128)S(1)}, f32[80,384]{1,0:T(8,128)}, u32[]{:S(2)}) copy-start(f32[80,384]{1,0:T(8,128)} %get-tuple-element.6) | copy-start | bytes 368644

commit v3 on v2

v3 whole, which is shorter than its diff:
```python
import jax
import jax.numpy as jnp
from jax import lax
from jax.experimental import pallas as pl
from jax.experimental.pallas import tpu as pltpu
from jax.sharding import PartitionSpec as P

F32, BF16 = jnp.float32, jnp.bfloat16
EPS = 1e-06
HD = 72
D = 1152
HALF = D // 2
FR = 16
PX = 16
TOK = FR * PX
FACTOR = HD**-0.5
NT = (((1,), (1,)), ((), ()))
TN = (((0,), (0,)), ((), ()))
QW, OW = 896, 384
MIB = 1 << 20


def dot(a, b, dims=None):
    if dims is None:
        return jnp.dot(a, b, preferred_element_type=F32)
    return lax.dot_general(a, b, dims, preferred_element_type=F32)


def to_rows(block):
    return jnp.concatenate([block[:, 8 * p : 8 * p + 8, :].reshape(128, D) for p in range(2)], axis=0)


def from_rows(rows):
    return jnp.concatenate([rows[128 * p : 128 * p + 128].reshape(FR, 8, D) for p in range(2)], axis=1)


def head_scale(v):
    return lax.rsqrt(jnp.sum(v * v, axis=0, keepdims=True) * (1.0 / HD) + EPS)


def forward_head(q, k, v, mask, keep):
    qn, kn, vb = (q * head_scale(q)).astype(BF16), (k * head_scale(k)).astype(BF16), v.astype(BF16)
    out = []
    for p in range(2):
        at = slice(128 * p, 128 * p + 128)
        e = jnp.exp(dot(kn[:, at], qn[:, at], TN) * FACTOR).reshape(FR, 8, 128)
        probs = (e * (mask / jnp.sum(e, axis=0))[None]).reshape(128, 128)
        keep(p, probs)
        out.append(dot(vb[:, at], probs.astype(BF16)))
    return jnp.concatenate(out, axis=1)


def backward_head(q, k, v, ga, probs_of):
    rq, rk = head_scale(q), head_scale(k)
    qn, kn = (q * rq).astype(BF16), (k * rk).astype(BF16)
    vb, gb = v.astype(BF16), ga.astype(BF16)
    out = []
    for p in range(2):
        at = slice(128 * p, 128 * p + 128)
        qh, kh, vh, gh = qn[:, at], kn[:, at], vb[:, at], gb[:, at]
        flat = probs_of(p)
        probs = flat.reshape(FR, 8, 128)
        pb = flat.astype(BF16)
        grad_probs = dot(vh, gh, TN).reshape(FR, 8, 128)
        total = jnp.sum(probs * grad_probs, axis=0)
        gs = (probs * (grad_probs - total[None]) * FACTOR).reshape(128, 128).astype(BF16)
        out.append((dot(kh, gs), dot(qh, gs, NT), dot(gh, pb, NT)))
    gqn, gkn, gv = (jnp.concatenate(pair, axis=1) for pair in zip(*out))
    tq = jnp.sum(gqn * q, axis=0, keepdims=True) * (1.0 / HD)
    tk = jnp.sum(gkn * k, axis=0, keepdims=True) * (1.0 / HD)
    gq = rq * gqn - q * (rq * rq * rq * tq)
    gk = rk * gkn - k * (rk * rk * rk * tk)
    return gq, gk, gv


def add(own, *others):
    value = own.astype(F32)
    for other in others:
        value = value + other.astype(F32)
    return value


def kernel(
    x_hbm, dout_hbm, wqkv_hbm, wout_hbm, back_ref, resq_ref, reso_ref,
    xv, wqkv, wout, up, std, proj, gat, probs, branch, hold, nt, nall, at, pa, ut, pu, gp, gall,
    ob, rob, tb, ub, sum_o, zs_o, zr_o, kept_o, hs_o, hr_o,
    s2, r2, sum_q, zs_q, zr_q, kept_q, hs_q, hr_q,
    load, sp_s, sp_r, pair_s, pair_r, bk_s, bk_r, n_s, n_r, gx_s, gx_r, fw_s, fw_r,
    ob_s, ob_r, y_s, y_r, x2_s, x2_r, z_s, z_r,
):
    dp, seq = lax.axis_index("dp"), lax.axis_index("seq")
    y, zl, core, x, zh = dp // 4, (dp // 2) % 2, dp % 2, seq // 4, seq % 4

    def seq_peer(o):
        return {"seq": lax.rem(seq + o, 16)}

    def x_peer(o):
        return {"seq": lax.rem(x + o, 4) * 4 + zh}

    def zh_peer(o):
        return {"seq": x * 4 + lax.rem(zh + o, 4)}

    def y_peer(o):
        return {"dp": lax.rem(y + o, 4) * 4 + zl * 2 + core}

    core_peer = {"dp": dp + 1 - 2 * core}
    zl_peer = {"dp": dp + 2 - 4 * zl}

    def send(src, dst, s_sem, r_sem, peer):
        copy = pltpu.make_async_remote_copy(src_ref=src, dst_ref=dst, send_sem=s_sem, recv_sem=r_sem, device_id=peer)
        copy.start()
        return copy

    def wait(copies):
        for copy in copies:
            copy.wait()

    barrier = pltpu.get_barrier_semaphore()
    for peer in [seq_peer(o) for o in range(1, 16)] + [y_peer(o) for o in range(1, 4)] + [core_peer, zl_peer]:
        pl.semaphore_signal(barrier, inc=1, device_id=peer)
    loads = [
        pltpu.make_async_copy(x_hbm, xv, load.at[0]),
        pltpu.make_async_copy(wqkv_hbm, wqkv, load.at[1]),
        pltpu.make_async_copy(wout_hbm, wout, load.at[2]),
        pltpu.make_async_copy(dout_hbm.at[seq], up.at[seq], load.at[3]),
    ]
    for copy in loads:
        copy.start()
    pl.semaphore_wait(barrier, 20)
    order = (8, 7, 9, 6, 10, 5, 11, 4, 12, 3, 13, 2, 14, 1, 15)
    spread = [
        send(dout_hbm.at[lax.rem(seq + o, 16)], up.at[seq], sp_s.at[o], sp_r.at[o], seq_peer(o)) for o in order
    ]

    loads[0].wait()
    rows = to_rows(xv[...].astype(F32))
    centred = rows - jnp.mean(rows, axis=-1, keepdims=True)
    inverse = lax.rsqrt(jnp.mean(centred * centred, axis=-1, keepdims=True) + EPS)
    standard = centred * inverse
    std[...] = standard
    normed = standard.astype(BF16)
    standard_t = standard.T
    for c in range(2):
        nt[c] = jnp.concatenate(
            [standard_t[HD * (2 * b + c) : HD * (2 * b + c + 1)] for b in range(8)], axis=0
        ).astype(BF16)
    pair_n = send(nt.at[1 - core], nall.at[:, TOK : 2 * TOK], pair_s.at[0], pair_r.at[0], core_peer)
    nall[:, 0:TOK] = nt[core]
    right, left = x_peer(1), x_peer(3)
    loads[1].wait()
    for t in range(3):
        proj[D * t : D * t + D, :] = dot(normed, wqkv[:, D * t : D * t + D]).T
    pair_n.wait()
    both = nall.at[:, 0 : 2 * TOK]
    rows_r = send(both, nall.at[:, 2 * TOK : 4 * TOK], n_s.at[0], n_r.at[0], right)
    rows_l = send(both, nall.at[:, 6 * TOK : 8 * TOK], n_s.at[1], n_r.at[1], left)

    mask = (
        lax.broadcasted_iota(jnp.int32, (8, 128), 0) == lax.broadcasted_iota(jnp.int32, (8, 128), 1) % 8
    ).astype(F32)

    def forward_group(i, carry):
        base = pl.multiple_of(i * 288, 288)
        blocks = [proj[pl.ds(pl.multiple_of(D * t + base, 288), 288), :] for t in range(3)]
        heads = []
        for h in range(4):

            def keep(p, value, h=h):
                probs[i * 4 + h, p] = value

            heads.append(forward_head(*(b[HD * h : HD * h + HD] for b in blocks), mask, keep))
        half = pl.multiple_of(i * 144, 144)
        for c in range(2):
            at[c, pl.ds(half, 144), :] = jnp.concatenate([heads[c], heads[c + 2]], axis=0).astype(BF16)
        return carry

    lax.fori_loop(0, 4, forward_group, 0)
    pair_a = send(at.at[1 - core], pa, pair_s.at[1], pair_r.at[1], core_peer)

    loads[2].wait()
    loads[3].wait()
    wait(spread)
    up_t = to_rows(up[...].astype(F32)).T.astype(BF16)
    ut[...] = up_t
    pair_u = send(ut, pu, pair_s.at[2], pair_r.at[2], core_peer)
    gat[...] = dot(wout[...], up_t)
    wait([pair_a, pair_u])

    own_a = at[core]
    for n in range(3):
        cols = slice(OW * n, OW * n + OW)
        val = (dot(own_a, ut[cols, :], NT) + dot(pa[...], pu[cols, :], NT)).astype(BF16)
        for r in range(4):
            ob[r, :, cols] = val[144 * r : 144 * r + 144]
    out_y = [
        send(ob.at[lax.rem(y + o, 4)], rob.at[o - 1], ob_s.at[o - 1], ob_r.at[o - 1], y_peer(o)) for o in (2, 1, 3)
    ]
    wait([rows_r, rows_l])
    rows_on = [
        send(nall.at[:, 2 * TOK : 3 * TOK], nall.at[:, 4 * TOK : 5 * TOK], n_s.at[2], n_r.at[2], right),
        send(nall.at[:, 7 * TOK : 8 * TOK], nall.at[:, 5 * TOK : 6 * TOK], n_s.at[3], n_r.at[3], left),
    ]


    def columns(g, o, part):
        place = gall.at[pl.ds(pl.multiple_of(part * 288, 32), 288), pl.ds(pl.multiple_of(o * 2 * TOK, 2 * TOK), TOK)]
        return pltpu.make_async_remote_copy(
            src_ref=gp.at[pl.ds(pl.multiple_of(g * 288, 32), 288)],
            dst_ref=place,
            send_sem=gx_s.at[g],
            recv_sem=gx_r.at[(o - 1) * 3 + part],
            device_id=x_peer(o),
        )

    def backward_group(i, carry):
        base = pl.multiple_of(i * 288, 288)
        blocks = [proj[pl.ds(pl.multiple_of(D * t + base, 288), 288), :] for t in range(3)]
        blocks.append(gat[pl.ds(base, 288), :])
        heads = [
            backward_head(*(b[HD * h : HD * h + HD] for b in blocks), lambda p, h=h: probs[i * 4 + h, p])
            for h in range(4)
        ]
        for t in range(3):
            gp[pl.ds(pl.multiple_of(D * t + base, 288), 288), :] = jnp.concatenate(
                [h[t] for h in heads], axis=0
            ).astype(BF16)
            g = 4 * t + i
            o = lax.rem(g // 3 - x + 4, 4)

            @pl.when(o != 0)
            def _():
                columns(g, o, lax.rem(g, 3)).start()

        return carry

    lax.fori_loop(0, 4, backward_group, 0)
    mine = gp.at[pl.ds(pl.multiple_of(x * 864, 32), 864)]
    own_g = pltpu.make_async_copy(mine, gall.at[0:864, 0:TOK], load.at[4])
    own_g.start()
    pair_g = send(mine, gall.at[0:864, TOK : 2 * TOK], fw_s.at[9], fw_r.at[9], core_peer)

    gn = dot(wqkv[...], gp[...]).T
    standard = std[...]
    value = inverse * (
        gn
        - jnp.mean(gn, axis=-1, keepdims=True)
        - standard * jnp.mean(gn * standard, axis=-1, keepdims=True)
    )
    branch[...] = from_rows(value).astype(BF16).reshape(4, 4, PX, D)
    back_z = [
        send(branch.at[:, lax.rem(zh + o, 4)], hold.at[zh], bk_s.at[o - 1], bk_r.at[o - 1], zh_peer(o))
        for o in (2, 1, 3)
    ]
    hold[zh] = branch[:, zh]

    wait(out_y)
    val = add(ob[y], rob[0], rob[1], rob[2]).astype(BF16)
    for b in range(4):
        tb[b, :, 0:288] = val[:, 288 * b : 288 * b + 288]
        tb[b, :, 288:OW] = jnp.zeros((144, OW - 288), BF16)

    wait(rows_on + [pair_g])
    own_g.wait()
    sums_y = []
    for turn in range(3):
        part = lax.rem(turn + x, 3)
        rows = pl.ds(pl.multiple_of(part * 288, 32), 288)
        forwards = []
        for o in (1, 3, 2):
            columns(0, o, part).wait_recv()
            sem = (o - 1) * 3 + part
            forwards.append(
                send(
                    gall.at[rows, 2 * o * TOK : (2 * o + 1) * TOK],
                    gall.at[rows, (2 * o + 1) * TOK : (2 * o + 2) * TOK],
                    fw_s.at[sem], fw_r.at[sem], core_peer,
                )
            )
        if turn == 2:
            later = [
                send(tb.at[lax.rem(x + o, 4)], ub.at[o - 1], x2_s.at[o - 1], x2_r.at[o - 1], x_peer(o))
                for o in (2, 1, 3)
            ]
            wait(back_z)
            back_x = [
                send(
                    hold.at[:, lax.rem(x + o, 4)], back_ref.at[pl.ds(x * 4, 4)],
                    bk_s.at[o + 2], bk_r.at[o + 2], x_peer(o),
                )
                for o in (2, 1, 3)
            ]
            back_ref[pl.ds(x * 4, 4)] = hold[:, x]
        wait(forwards)
        val = dot(nall[...], gall[rows, :], NT)
        val = jnp.concatenate([val, jnp.zeros((HALF, OW - 288), F32)], axis=1).astype(BF16)
        for b in range(4):
            s2[b, part] = val[144 * b : 144 * b + 144]
        for o in (2, 1, 3):
            sem = 3 * turn + o - 1
            sums_y.append(
                send(s2.at[lax.rem(y + o, 4), part], r2.at[o - 1, part], y_s.at[sem], y_r.at[sem], y_peer(o))
            )
    for o in range(1, 4):
        for part in range(3):
            columns(3 * lax.rem(x + o, 4) + part, o, part).wait_send()

    def pair_z(sums, zs, zr, sem):
        zs[...] = sums[pl.ds(pl.multiple_of(64 * (1 - zl), 64), 80), :].astype(BF16)
        return send(zs, zr, z_s.at[sem], z_r.at[sem], zl_peer)

    def four_z(pair, sums, zr, kept, hs, hr, width, sem):
        pair.wait()
        kept[...] = sums[pl.ds(pl.multiple_of(64 * zl, 64), 80), :] + zr[...].astype(F32)
        value = kept[pl.ds(pl.multiple_of(8 * zl, 8), 72), :]
        hs[...] = jnp.zeros_like(hs)
        for b in range(4):
            hs[b, 0:72, 0:width] = value[:, width * b : width * b + width].astype(BF16)
        return [
            send(hs.at[lax.rem(zh + o, 4)], hr.at[o - 1], z_s.at[sem + o], z_r.at[sem + o], zh_peer(o))
            for o in (2, 1, 3)
        ]

    wait(later)
    sum_o[...] = add(tb[x], ub[0], ub[1], ub[2])
    pair_o = pair_z(sum_o, zs_o, zr_o, 0)
    wait(sums_y)
    val = add(s2[y], r2[0], r2[1], r2[2])
    sum_q[...] = jnp.concatenate([val[0, :, 0:288], val[1, :, 0:288], val[2, :, 0:288], jnp.zeros((144, 32), F32)], axis=1)
    pair_q = pair_z(sum_q, zs_q, zr_q, 4)
    four_o = four_z(pair_o, sum_o, zr_o, kept_o, hs_o, hr_o, 72, 0)
    four_q = four_z(pair_q, sum_q, zr_q, kept_q, hs_q, hr_q, 216, 4)
    wait(four_o)
    reso_ref[...] = add(hs_o[zh], hr_o[0], hr_o[1], hr_o[2])
    wait(back_x)
    wait(four_q)
    resq_ref[...] = add(hs_q[zh], hr_q[0], hr_q[1], hr_q[2])


def fused(x, dout, wqkv, wout):
    dma = pltpu.SemaphoreType.DMA

    def buf(*shape, dtype=BF16):
        return pltpu.VMEM(shape, dtype)

    return pl.pallas_call(
        kernel,
        out_shape=[
            jax.ShapeDtypeStruct((16, PX, D), BF16),
            jax.ShapeDtypeStruct((80, 256), F32),
            jax.ShapeDtypeStruct((80, 128), F32),
        ],
        in_specs=[pl.BlockSpec(memory_space=pl.ANY)] * 4,
        out_specs=[pl.BlockSpec(memory_space=pltpu.VMEM)] * 3,
        scratch_shapes=[
            buf(FR, PX, D), buf(D, 3 * D), buf(D, D), buf(16, PX, D),
            buf(TOK, D, dtype=F32), buf(3 * D, TOK, dtype=F32), buf(D, TOK, dtype=F32),
            buf(16, 2, 128, 128, dtype=F32), buf(4, 4, PX, D), buf(4, 4, PX, D),
            buf(2, HALF, TOK), buf(HALF, 8 * TOK), buf(2, HALF, TOK), buf(HALF, TOK),
            buf(D, TOK), buf(D, TOK), buf(3 * D, TOK), buf(864, 8 * TOK),
            buf(4, 144, D), buf(3, 144, D), buf(4, 144, OW), buf(3, 144, OW),
            buf(144, OW, dtype=F32), buf(80, OW), buf(80, OW), buf(80, OW, dtype=F32),
            buf(4, 80, 128), buf(3, 80, 128),
            buf(4, 3, 144, OW), buf(3, 3, 144, OW),
            buf(144, QW, dtype=F32), buf(80, QW), buf(80, QW), buf(80, QW, dtype=F32),
            buf(4, 80, 256), buf(3, 80, 256),
            dma((5,)), dma((16,)), dma((16,)), dma((3,)), dma((3,)), dma((6,)), dma((6,)),
            dma((4,)), dma((4,)), dma((12,)), dma((9,)), dma((10,)), dma((10,)),
            dma((3,)), dma((3,)), dma((9,)), dma((9,)), dma((3,)), dma((3,)), dma((8,)), dma((8,)),
        ],
        compiler_params=pltpu.CompilerParams(
            collective_id=1, has_side_effects=True, vmem_limit_bytes=56 * MIB
        ),
    )(x, dout, wqkv, wout)


def finish_kernel(dout, back, resq, reso, d_x1, g_qkv, g_out):
    d_x1[...] = (dout[...].astype(F32) + back[...].astype(F32)).astype(BF16)
    g_qkv[...] = resq[0:72, 0:216] * (1.0 / 256.0)
    g_out[...] = reso[0:72, 0:72] * (1.0 / 256.0)


def finish(dout, back, resq, reso):
    vmem = pl.BlockSpec(memory_space=pltpu.VMEM)
    return pl.pallas_call(
        finish_kernel,
        out_shape=[
            jax.ShapeDtypeStruct((16, PX, D), BF16),
            jax.ShapeDtypeStruct((72, 216), F32),
            jax.ShapeDtypeStruct((72, 72), F32),
        ],
        in_specs=[vmem] * 4,
        out_specs=[vmem] * 3,
    )(dout, back, resq, reso)


def local(x1_pixels, dout_frames, w_qkv, w_out):
    x = x1_pixels.reshape(FR, PX, D)
    dout = dout_frames.reshape(16, PX, D)
    back, resq, reso = fused(x, dout, w_qkv, w_out)
    d_x1, g_qkv, g_out = finish(dout, back, resq, reso)
    return d_x1.reshape(dout_frames.shape), g_qkv, g_out


def solution(mesh):
    return jax.shard_map(
        local,
        mesh=mesh,
        in_specs=(P("dp", None, "seq", None), P("dp", "seq", None, None), P(), P()),
        out_specs=(P("dp", "seq", None, None), P("dp", "seq"), P("dp", "seq")),
        check_vma=False,
    )
```

time: 101 us -> 90.8 us (0.90)
  Pallas kernels: 97.1 us -> 90.1 us
  other arithmetic: 2.06 us -> 0 us
  local copies, waits for them, and re-layouts: 1.27 us -> 0 us
    pallas_call x1, Pallas kernels: 97.1 us -> 87.8 us  [fused(): pl.pallas_call(kernel, out_shape=[jax.ShapeDtypeStruct((16, PX, D), BF16)...]
    pallas_call x0 -> x1, Pallas kernels: none -> 2.21 us  [finish(): pl.pallas_call(finish_kernel, out_shape=[jax.ShapeDtypeStruct((16, PX, D)...]
    convert_element_type x1 -> x0, other arithmetic: 2.05 us -> none  [local(): (dout.astype(F32) + back.astype(F32)).astype(BF16)]
    slice x2 -> x0, local copies, waits for them, and re-layouts: 1.26 us -> none  [local(): return (d_x1, res[0:72, 0:216], res[0:72, 256:328])]
where the time goes in v3:
time: 90.8 us; the launch traced here: 90.7 us
  Pallas kernels  90.1 us (99%)
    pallas_call x1, Pallas kernels, fused(): pl.pallas_call(kernel, out_shape=[jax.ShapeDtypeStruct((16, PX, D), BF16)...  87.8 us
    pallas_call x1, Pallas kernels, finish(): pl.pallas_call(finish_kernel, out_shape=[jax.ShapeDtypeStruct((16, PX, D)...  2.21 us

profile of v3, /device:TPU:32, one launch (start us, length us, event | category | flops | bytes accessed | tf_op | source)
XLA Modules:
  0.0 90.7 jit_solution(9473873497599476997)
XLA Ops:
  0.6 87.8 %shard_map.67 = (bf16[16,16,1152]{2,1,0:T(8,128)(2,1)}, f32[80,256]{1,0:T(8,128)}, f32[80,128]{1,0:T(8,128)}) custom-call(bf16[16,16,1152]{2,1,0:T(8,128)(2,1)} %bitcast.5, bf16[16,16,1152]{2,1,0:T(8,128)(2,1)} %bitcast.3, bf16[1152,3456]{1,0:T(8,128)(2,1)} %wqkv_hbm.1, bf16[1152,1152]{1,0:T(8,128)(2,1)} %wout_hbm.1), custom_call_target="tpu_custom_call" | custom-call | tf_op jit(solution)/shard_map/pallas_call | solution.py:345
  88.5 2.2 %shard_map.68 = (bf16[16,16,1152]{2,1,0:T(8,128)(2,1)}, f32[72,216]{1,0:T(8,128)}, f32[72,72]{1,0:T(8,128)}) custom-call(bf16[16,16,1152]{2,1,0:T(8,128)(2,1)} %bitcast.4, bf16[16,16,1152]{2,1,0:T(8,128)(2,1)} %get-tuple-element.9.back, f32[80,256]{1,0:T(8,128)} %get-tuple-element.10.resq, f32[80,128]{1,0:T(8,128)} %get-tuple-element.11.reso), custom_call_target="tpu_custom_call" | custom-call | tf_op jit(solution)/shard_map/pallas_call | solution.py:384

commit v4 on v3

--- a/solution.py
+++ b/solution.py
@@ -81,8 +81,8 @@
 
 
 def kernel(
-    x_hbm, dout_hbm, wqkv_hbm, wout_hbm, back_ref, resq_ref, reso_ref,
-    xv, wqkv, wout, up, std, proj, gat, probs, branch, hold, nt, nall, at, pa, ut, pu, gp, gall,
+    x_hbm, dout_hbm, wqkv_hbm, wout_hbm, d_x1_ref, resq_ref, reso_ref,
+    xv, wqkv, wout, up, std, proj, gat, probs, branch, hold, back, nt, nall, at, pa, ut, pu, gp, gall,
     ob, rob, tb, ub, sum_o, zs_o, zr_o, kept_o, hs_o, hr_o,
     s2, r2, sum_q, zs_q, zr_q, kept_q, hs_q, hr_q,
     load, sp_s, sp_r, pair_s, pair_r, bk_s, bk_r, n_s, n_r, gx_s, gx_r, fw_s, fw_r,
@@ -147,13 +147,13 @@
     pair_n = send(nt.at[1 - core], nall.at[:, TOK : 2 * TOK], pair_s.at[0], pair_r.at[0], core_peer)
     nall[:, 0:TOK] = nt[core]
     right, left = x_peer(1), x_peer(3)
-    loads[1].wait()
-    for t in range(3):
-        proj[D * t : D * t + D, :] = dot(normed, wqkv[:, D * t : D * t + D]).T
     pair_n.wait()
     both = nall.at[:, 0 : 2 * TOK]
     rows_r = send(both, nall.at[:, 2 * TOK : 4 * TOK], n_s.at[0], n_r.at[0], right)
     rows_l = send(both, nall.at[:, 6 * TOK : 8 * TOK], n_s.at[1], n_r.at[1], left)
+    loads[1].wait()
+    for t in range(3):
+        proj[D * t : D * t + D, :] = dot(normed, wqkv[:, D * t : D * t + D]).T
 
     mask = (
         lax.broadcasted_iota(jnp.int32, (8, 128), 0) == lax.broadcasted_iota(jnp.int32, (8, 128), 1) % 8
@@ -176,6 +176,9 @@
 
     lax.fori_loop(0, 4, forward_group, 0)
     pair_a = send(at.at[1 - core], pa, pair_s.at[1], pair_r.at[1], core_peer)
+
+    hs_o[...] = jnp.zeros_like(hs_o)
+    hs_q[...] = jnp.zeros_like(hs_q)
 
     loads[2].wait()
     loads[3].wait()
@@ -202,15 +205,20 @@
     ]
 
 
-    def columns(g, o, part):
-        place = gall.at[pl.ds(pl.multiple_of(part * 288, 32), 288), pl.ds(pl.multiple_of(o * 2 * TOK, 2 * TOK), TOK)]
+    def columns(o, turn):
+        xd = lax.rem(x + o, 4)
+        part = lax.rem(turn + xd, 3)
         return pltpu.make_async_remote_copy(
-            src_ref=gp.at[pl.ds(pl.multiple_of(g * 288, 32), 288)],
-            dst_ref=place,
-            send_sem=gx_s.at[g],
-            recv_sem=gx_r.at[(o - 1) * 3 + part],
+            src_ref=gp.at[pl.ds(pl.multiple_of((3 * xd + part) * 288, 32), 288)],
+            dst_ref=gall.at[pl.ds(pl.multiple_of(part * 288, 32), 288), 2 * o * TOK : (2 * o + 1) * TOK],
+            send_sem=gx_s.at[3 * (o - 1) + turn],
+            recv_sem=gx_r.at[3 * (o - 1) + turn],
             device_id=x_peer(o),
         )
+
+    def issue(turn):
+        for o in (2, 1, 3):
+            columns(o, turn).start()
 
     def backward_group(i, carry):
         base = pl.multiple_of(i * 288, 288)
@@ -224,16 +232,12 @@
             gp[pl.ds(pl.multiple_of(D * t + base, 288), 288), :] = jnp.concatenate(
                 [h[t] for h in heads], axis=0
             ).astype(BF16)
-            g = 4 * t + i
-            o = lax.rem(g // 3 - x + 4, 4)
-
-            @pl.when(o != 0)
-            def _():
-                columns(g, o, lax.rem(g, 3)).start()
-
         return carry
 
-    lax.fori_loop(0, 4, backward_group, 0)
+    lax.fori_loop(0, 2, backward_group, 0)
+    issue(0)
+    lax.fori_loop(2, 4, backward_group, 0)
+    issue(1)
     mine = gp.at[pl.ds(pl.multiple_of(x * 864, 32), 864)]
     own_g = pltpu.make_async_copy(mine, gall.at[0:864, 0:TOK], load.at[4])
     own_g.start()
@@ -253,22 +257,38 @@
     ]
     hold[zh] = branch[:, zh]
 
+    for o in (2, 1, 3):
+        columns(o, 0).wait_send()
+    issue(2)
+
     wait(out_y)
     val = add(ob[y], rob[0], rob[1], rob[2]).astype(BF16)
     for b in range(4):
         tb[b, :, 0:288] = val[:, 288 * b : 288 * b + 288]
         tb[b, :, 288:OW] = jnp.zeros((144, OW - 288), BF16)
 
+    own_d = pltpu.make_async_copy(dout_hbm, up, load.at[3])
+    own_d.start()
+
     wait(rows_on + [pair_g])
     own_g.wait()
     sums_y = []
+
+    def pair_z(turn):
+        wait(sums_y[turn])
+        part = lax.rem(turn + x, 3)
+        sum_q[part] = add(s2[y, part], r2[0, part], r2[1, part], r2[2, part])
+        zs_q[part] = sum_q[part, pl.ds(pl.multiple_of(64 * (1 - zl), 64), 80), :].astype(BF16)
+        return send(zs_q.at[part], zr_q.at[part], z_s.at[turn + 4], z_r.at[turn + 4], zl_peer)
+
+    pairs_q = []
     for turn in range(3):
         part = lax.rem(turn + x, 3)
         rows = pl.ds(pl.multiple_of(part * 288, 32), 288)
         forwards = []
         for o in (1, 3, 2):
-            columns(0, o, part).wait_recv()
-            sem = (o - 1) * 3 + part
+            columns(o, turn).wait_recv()
+            sem = (o - 1) * 3 + turn
             forwards.append(
                 send(
                     gall.at[rows, 2 * o * TOK : (2 * o + 1) * TOK],
@@ -276,43 +296,45 @@
                     fw_s.at[sem], fw_r.at[sem], core_peer,
                 )
             )
-        if turn == 2:
-            later = [
-                send(tb.at[lax.rem(x + o, 4)], ub.at[o - 1], x2_s.at[o - 1], x2_r.at[o - 1], x_peer(o))
-                for o in (2, 1, 3)
-            ]
-            wait(back_z)
-            back_x = [
-                send(
-                    hold.at[:, lax.rem(x + o, 4)], back_ref.at[pl.ds(x * 4, 4)],
-                    bk_s.at[o + 2], bk_r.at[o + 2], x_peer(o),
-                )
-                for o in (2, 1, 3)
-            ]
-            back_ref[pl.ds(x * 4, 4)] = hold[:, x]
         wait(forwards)
         val = dot(nall[...], gall[rows, :], NT)
         val = jnp.concatenate([val, jnp.zeros((HALF, OW - 288), F32)], axis=1).astype(BF16)
         for b in range(4):
             s2[b, part] = val[144 * b : 144 * b + 144]
-        for o in (2, 1, 3):
-            sem = 3 * turn + o - 1
-            sums_y.append(
-                send(s2.at[lax.rem(y + o, 4), part], r2.at[o - 1, part], y_s.at[sem], y_r.at[sem], y_peer(o))
-            )
-    for o in range(1, 4):
-        for part in range(3):
-            columns(3 * lax.rem(x + o, 4) + part, o, part).wait_send()
-
-    def pair_z(sums, zs, zr, sem):
-        zs[...] = sums[pl.ds(pl.multiple_of(64 * (1 - zl), 64), 80), :].astype(BF16)
-        return send(zs, zr, z_s.at[sem], z_r.at[sem], zl_peer)
-
-    def four_z(pair, sums, zr, kept, hs, hr, width, sem):
-        pair.wait()
-        kept[...] = sums[pl.ds(pl.multiple_of(64 * zl, 64), 80), :] + zr[...].astype(F32)
-        value = kept[pl.ds(pl.multiple_of(8 * zl, 8), 72), :]
-        hs[...] = jnp.zeros_like(hs)
+        sums_y.append(
+            [
+                send(
+                    s2.at[lax.rem(y + o, 4), part], r2.at[o - 1, part],
+                    y_s.at[3 * turn + o - 1], y_r.at[3 * turn + o - 1], y_peer(o),
+                )
+                for o in (2, 1, 3)
+            ]
+        )
+        if turn == 1:
+            pairs_q.append(pair_z(0))
+    for o in (2, 1, 3):
+        columns(o, 1).wait_send()
+        columns(o, 2).wait_send()
+    later = [
+        send(tb.at[lax.rem(x + o, 4)], ub.at[o - 1], x2_s.at[o - 1], x2_r.at[o - 1], x_peer(o)) for o in (2, 1, 3)
+    ]
+    wait(back_z)
+    back_x = [
+        send(
+            hold.at[:, lax.rem(x + o, 4)], back.at[pl.ds(x * 4, 4)], bk_s.at[o + 2], bk_r.at[o + 2], x_peer(o)
+        )
+        for o in (2, 1, 3)
+    ]
+    back[pl.ds(x * 4, 4)] = hold[:, x]
+    pairs_q.append(pair_z(1))
+
+    wait(later)
+    sum_o[...] = add(tb[x], ub[0], ub[1], ub[2])
+    zs_o[...] = sum_o[pl.ds(pl.multiple_of(64 * (1 - zl), 64), 80), :].astype(BF16)
+    pair_o = send(zs_o, zr_o, z_s.at[0], z_r.at[0], zl_peer)
+    pairs_q.append(pair_z(2))
+
+    def four_z(value, hs, hr, width, sem):
         for b in range(4):
             hs[b, 0:72, 0:width] = value[:, width * b : width * b + width].astype(BF16)
         return [
@@ -320,18 +342,20 @@
             for o in (2, 1, 3)
         ]
 
-    wait(later)
-    sum_o[...] = add(tb[x], ub[0], ub[1], ub[2])
-    pair_o = pair_z(sum_o, zs_o, zr_o, 0)
-    wait(sums_y)
-    val = add(s2[y], r2[0], r2[1], r2[2])
-    sum_q[...] = jnp.concatenate([val[0, :, 0:288], val[1, :, 0:288], val[2, :, 0:288], jnp.zeros((144, 32), F32)], axis=1)
-    pair_q = pair_z(sum_q, zs_q, zr_q, 4)
-    four_o = four_z(pair_o, sum_o, zr_o, kept_o, hs_o, hr_o, 72, 0)
-    four_q = four_z(pair_q, sum_q, zr_q, kept_q, hs_q, hr_q, 216, 4)
+    window = pl.ds(pl.multiple_of(64 * zl, 64), 80)
+    inner = pl.ds(pl.multiple_of(8 * zl, 8), 72)
+    pair_o.wait()
+    kept_o[...] = sum_o[window, :] + zr_o[...].astype(F32)
+    four_o = four_z(kept_o[inner, :], hs_o, hr_o, 72, 0)
+    wait(pairs_q)
+    for part in range(3):
+        kept_q[part] = sum_q[part, window, :] + zr_q[part].astype(F32)
+    four_q = four_z(jnp.concatenate([kept_q[part, inner, 0:288] for part in range(3)], axis=1), hs_q, hr_q, 216, 6)
+    wait(back_x)
+    own_d.wait()
+    d_x1_ref[...] = (up[...].astype(F32) + back[...].astype(F32)).astype(BF16)
     wait(four_o)
     reso_ref[...] = add(hs_o[zh], hr_o[0], hr_o[1], hr_o[2])
-    wait(back_x)
     wait(four_q)
     resq_ref[...] = add(hs_q[zh], hr_q[0], hr_q[1], hr_q[2])
 
@@ -354,18 +378,18 @@
         scratch_shapes=[
             buf(FR, PX, D), buf(D, 3 * D), buf(D, D), buf(16, PX, D),
             buf(TOK, D, dtype=F32), buf(3 * D, TOK, dtype=F32), buf(D, TOK, dtype=F32),
-            buf(16, 2, 128, 128, dtype=F32), buf(4, 4, PX, D), buf(4, 4, PX, D),
+            buf(16, 2, 128, 128, dtype=F32), buf(4, 4, PX, D), buf(4, 4, PX, D), buf(16, PX, D),
             buf(2, HALF, TOK), buf(HALF, 8 * TOK), buf(2, HALF, TOK), buf(HALF, TOK),
             buf(D, TOK), buf(D, TOK), buf(3 * D, TOK), buf(864, 8 * TOK),
             buf(4, 144, D), buf(3, 144, D), buf(4, 144, OW), buf(3, 144, OW),
             buf(144, OW, dtype=F32), buf(80, OW), buf(80, OW), buf(80, OW, dtype=F32),
             buf(4, 80, 128), buf(3, 80, 128),
             buf(4, 3, 144, OW), buf(3, 3, 144, OW),
-            buf(144, QW, dtype=F32), buf(80, QW), buf(80, QW), buf(80, QW, dtype=F32),
+            buf(3, 144, OW, dtype=F32), buf(3, 80, OW), buf(3, 80, OW), buf(3, 80, OW, dtype=F32),
             buf(4, 80, 256), buf(3, 80, 256),
             dma((5,)), dma((16,)), dma((16,)), dma((3,)), dma((3,)), dma((6,)), dma((6,)),
-            dma((4,)), dma((4,)), dma((12,)), dma((9,)), dma((10,)), dma((10,)),
-            dma((3,)), dma((3,)), dma((9,)), dma((9,)), dma((3,)), dma((3,)), dma((8,)), dma((8,)),
+            dma((4,)), dma((4,)), dma((9,)), dma((9,)), dma((10,)), dma((10,)),
+            dma((3,)), dma((3,)), dma((9,)), dma((9,)), dma((3,)), dma((3,)), dma((10,)), dma((10,)),
         ],
         compiler_params=pltpu.CompilerParams(
             collective_id=1, has_side_effects=True, vmem_limit_bytes=56 * MIB
@@ -373,13 +397,13 @@
     )(x, dout, wqkv, wout)
 
 
-def finish_kernel(dout, back, resq, reso, d_x1, g_qkv, g_out):
-    d_x1[...] = (dout[...].astype(F32) + back[...].astype(F32)).astype(BF16)
+def finish_kernel(d_x1, resq, reso, out, g_qkv, g_out):
+    out[...] = d_x1[...]
     g_qkv[...] = resq[0:72, 0:216] * (1.0 / 256.0)
     g_out[...] = reso[0:72, 0:72] * (1.0 / 256.0)
 
 
-def finish(dout, back, resq, reso):
+def finish(d_x1, resq, reso):
     vmem = pl.BlockSpec(memory_space=pltpu.VMEM)
     return pl.pallas_call(
         finish_kernel,
@@ -388,16 +412,15 @@
             jax.ShapeDtypeStruct((72, 216), F32),
             jax.ShapeDtypeStruct((72, 72), F32),
         ],
-        in_specs=[vmem] * 4,
+        in_specs=[vmem] * 3,
         out_specs=[vmem] * 3,
-    )(dout, back, resq, reso)
+    )(d_x1, resq, reso)
 
 
 def local(x1_pixels, dout_frames, w_qkv, w_out):
     x = x1_pixels.reshape(FR, PX, D)
     dout = dout_frames.reshape(16, PX, D)
-    back, resq, reso = fused(x, dout, w_qkv, w_out)
-    d_x1, g_qkv, g_out = finish(dout, back, resq, reso)
+    d_x1, g_qkv, g_out = finish(*fused(x, dout, w_qkv, w_out))
     return d_x1.reshape(dout_frames.shape), g_qkv, g_out
 
 

time: 90.8 us -> 88.1 us (0.970)
  Pallas kernels: 90.1 us -> 86.6 us
    pallas_call x1, Pallas kernels: 87.8 us -> 84.6 us  [fused(): pl.pallas_call(kernel, out_shape=[jax.ShapeDtypeStruct((16, PX, D), BF16)...]
where the time goes in v4:
time: 88.1 us; the launch traced here: 87.2 us
  Pallas kernels  86.6 us (98%)
    pallas_call x1, Pallas kernels, fused(): pl.pallas_call(kernel, out_shape=[jax.ShapeDtypeStruct((16, PX, D), BF16)...  84.6 us
    pallas_call x1, Pallas kernels, finish(): pl.pallas_call(finish_kernel, out_shape=[jax.ShapeDtypeStruct((16, PX, D)...  1.98 us

profile of v4, /device:TPU:32, one launch (start us, length us, event | category | flops | bytes accessed | tf_op | source)
XLA Modules:
  0.0 87.2 jit_solution(3740010547517385011)
XLA Ops:
  0.6 84.6 %shard_map.67 = (bf16[16,16,1152]{2,1,0:T(8,128)(2,1)}, f32[80,256]{1,0:T(8,128)}, f32[80,128]{1,0:T(8,128)}) custom-call(bf16[16,16,1152]{2,1,0:T(8,128)(2,1)} %bitcast.3, bf16[16,16,1152]{2,1,0:T(8,128)(2,1)} %bitcast.4, bf16[1152,3456]{1,0:T(8,128)(2,1)} %wqkv_hbm.1, bf16[1152,1152]{1,0:T(8,128)(2,1)} %wout_hbm.1), custom_call_target="tpu_custom_call" | custom-call | tf_op jit(solution)/shard_map/pallas_call | solution.py:369
  85.2 2.0 %shard_map.68 = (bf16[16,16,1152]{2,1,0:T(8,128)(2,1)}, f32[72,216]{1,0:T(8,128)}, f32[72,72]{1,0:T(8,128)}) custom-call(bf16[16,16,1152]{2,1,0:T(8,128)(2,1)} %get-tuple-element.9.d_x1, f32[80,256]{1,0:T(8,128)} %get-tuple-element.10.resq, f32[80,128]{1,0:T(8,128)} %get-tuple-element.11.reso), custom_call_target="tpu_custom_call" | custom-call | tf_op jit(solution)/shard_map/pallas_call | solution.py:408

commit v5 on v4

--- a/solution.py
+++ b/solution.py
@@ -84,9 +84,9 @@
     x_hbm, dout_hbm, wqkv_hbm, wout_hbm, d_x1_ref, resq_ref, reso_ref,
     xv, wqkv, wout, up, std, proj, gat, probs, branch, hold, back, nt, nall, at, pa, ut, pu, gp, gall,
     ob, rob, tb, ub, sum_o, zs_o, zr_o, kept_o, hs_o, hr_o,
-    s2, r2, sum_q, zs_q, zr_q, kept_q, hs_q, hr_q,
+    s2, r2, r3, sum_q, zs_q, zr_q, kept_q, hs_q, hr_q,
     load, sp_s, sp_r, pair_s, pair_r, bk_s, bk_r, n_s, n_r, gx_s, gx_r, fw_s, fw_r,
-    ob_s, ob_r, y_s, y_r, x2_s, x2_r, z_s, z_r,
+    ob_s, ob_r, y_s, y_r, d_s, d_r, x2_s, x2_r, z_s, z_r,
 ):
     dp, seq = lax.axis_index("dp"), lax.axis_index("seq")
     y, zl, core, x, zh = dp // 4, (dp // 2) % 2, dp % 2, seq // 4, seq % 4
@@ -116,7 +116,8 @@
             copy.wait()
 
     barrier = pltpu.get_barrier_semaphore()
-    for peer in [seq_peer(o) for o in range(1, 16)] + [y_peer(o) for o in range(1, 4)] + [core_peer, zl_peer]:
+    across = [{"dp": lax.rem(y + o, 4) * 4 + 2 * (1 - zl) + core} for o in range(1, 4)]
+    for peer in [seq_peer(o) for o in range(1, 16)] + [y_peer(o) for o in range(1, 4)] + across + [core_peer, zl_peer]:
         pl.semaphore_signal(barrier, inc=1, device_id=peer)
     loads = [
         pltpu.make_async_copy(x_hbm, xv, load.at[0]),
@@ -126,7 +127,7 @@
     ]
     for copy in loads:
         copy.start()
-    pl.semaphore_wait(barrier, 20)
+    pl.semaphore_wait(barrier, 23)
     order = (8, 7, 9, 6, 10, 5, 11, 4, 12, 3, 13, 2, 14, 1, 15)
     spread = [
         send(dout_hbm.at[lax.rem(seq + o, 16)], up.at[seq], sp_s.at[o], sp_r.at[o], seq_peer(o)) for o in order
@@ -148,9 +149,11 @@
     nall[:, 0:TOK] = nt[core]
     right, left = x_peer(1), x_peer(3)
     pair_n.wait()
-    both = nall.at[:, 0 : 2 * TOK]
-    rows_r = send(both, nall.at[:, 2 * TOK : 4 * TOK], n_s.at[0], n_r.at[0], right)
-    rows_l = send(both, nall.at[:, 6 * TOK : 8 * TOK], n_s.at[1], n_r.at[1], left)
+    own_rows, pair_rows = nall.at[:, 0:TOK], nall.at[:, TOK : 2 * TOK]
+    rows_first = [
+        send(own_rows, nall.at[:, 2 * TOK : 3 * TOK], n_s.at[0], n_r.at[0], right),
+        send(pair_rows, nall.at[:, 7 * TOK : 8 * TOK], n_s.at[1], n_r.at[1], left),
+    ]
     loads[1].wait()
     for t in range(3):
         proj[D * t : D * t + D, :] = dot(normed, wqkv[:, D * t : D * t + D]).T
@@ -177,6 +180,13 @@
     lax.fori_loop(0, 4, forward_group, 0)
     pair_a = send(at.at[1 - core], pa, pair_s.at[1], pair_r.at[1], core_peer)
 
+    wait(rows_first)
+    rows_on = [
+        send(nall.at[:, 2 * TOK : 3 * TOK], nall.at[:, 4 * TOK : 5 * TOK], n_s.at[2], n_r.at[2], right),
+        send(nall.at[:, 7 * TOK : 8 * TOK], nall.at[:, 5 * TOK : 6 * TOK], n_s.at[3], n_r.at[3], left),
+        send(pair_rows, nall.at[:, 3 * TOK : 4 * TOK], n_s.at[4], n_r.at[4], right),
+        send(own_rows, nall.at[:, 6 * TOK : 7 * TOK], n_s.at[5], n_r.at[5], left),
+    ]
     hs_o[...] = jnp.zeros_like(hs_o)
     hs_q[...] = jnp.zeros_like(hs_q)
 
@@ -197,11 +207,6 @@
             ob[r, :, cols] = val[144 * r : 144 * r + 144]
     out_y = [
         send(ob.at[lax.rem(y + o, 4)], rob.at[o - 1], ob_s.at[o - 1], ob_r.at[o - 1], y_peer(o)) for o in (2, 1, 3)
-    ]
-    wait([rows_r, rows_l])
-    rows_on = [
-        send(nall.at[:, 2 * TOK : 3 * TOK], nall.at[:, 4 * TOK : 5 * TOK], n_s.at[2], n_r.at[2], right),
-        send(nall.at[:, 7 * TOK : 8 * TOK], nall.at[:, 5 * TOK : 6 * TOK], n_s.at[3], n_r.at[3], left),
     ]
 
 
@@ -301,23 +306,30 @@
         val = jnp.concatenate([val, jnp.zeros((HALF, OW - 288), F32)], axis=1).astype(BF16)
         for b in range(4):
             s2[b, part] = val[144 * b : 144 * b + 144]
-        sums_y.append(
-            [
-                send(
-                    s2.at[lax.rem(y + o, 4), part], r2.at[o - 1, part],
-                    y_s.at[3 * turn + o - 1], y_r.at[3 * turn + o - 1], y_peer(o),
-                )
-                for o in (2, 1, 3)
-            ]
-        )
+        if turn < 2:
+            sums_y.append(
+                [
+                    send(
+                        s2.at[lax.rem(y + o, 4), part], r2.at[o - 1, part],
+                        y_s.at[3 * turn + o - 1], y_r.at[3 * turn + o - 1], y_peer(o),
+                    )
+                    for o in (2, 1, 3)
+                ]
+            )
         if turn == 1:
             pairs_q.append(pair_z(0))
+            later = [
+                send(tb.at[lax.rem(x + o, 4)], ub.at[o - 1], x2_s.at[o - 1], x2_r.at[o - 1], x_peer(o)) for o in (2, 1, 3)
+            ]
+    last = lax.rem(2 + x, 3)
+    direct = []
+    for o, oz in ((2, 1), (2, 0), (1, 1), (1, 0), (3, 1), (3, 0), (0, 1)):
+        yd, zd, sem = lax.rem(y + o, 4), (zl if oz == 0 else 1 - zl), 2 * o + oz - 1
+        piece = s2.at[yd, last, pl.ds(pl.multiple_of(64 * zd, 64), 80)]
+        direct.append(send(piece, r3.at[sem], d_s.at[sem], d_r.at[sem], {"dp": yd * 4 + zd * 2 + core}))
     for o in (2, 1, 3):
         columns(o, 1).wait_send()
         columns(o, 2).wait_send()
-    later = [
-        send(tb.at[lax.rem(x + o, 4)], ub.at[o - 1], x2_s.at[o - 1], x2_r.at[o - 1], x_peer(o)) for o in (2, 1, 3)
-    ]
     wait(back_z)
     back_x = [
         send(
@@ -332,7 +344,6 @@
     sum_o[...] = add(tb[x], ub[0], ub[1], ub[2])
     zs_o[...] = sum_o[pl.ds(pl.multiple_of(64 * (1 - zl), 64), 80), :].astype(BF16)
     pair_o = send(zs_o, zr_o, z_s.at[0], z_r.at[0], zl_peer)
-    pairs_q.append(pair_z(2))
 
     def four_z(value, hs, hr, width, sem):
         for b in range(4):
@@ -348,8 +359,11 @@
     kept_o[...] = sum_o[window, :] + zr_o[...].astype(F32)
     four_o = four_z(kept_o[inner, :], hs_o, hr_o, 72, 0)
     wait(pairs_q)
-    for part in range(3):
+    for turn in range(2):
+        part = lax.rem(turn + x, 3)
         kept_q[part] = sum_q[part, window, :] + zr_q[part].astype(F32)
+    wait(direct)
+    kept_q[last] = add(s2[y, last, window, :], *(r3[n] for n in range(7)))
     four_q = four_z(jnp.concatenate([kept_q[part, inner, 0:288] for part in range(3)], axis=1), hs_q, hr_q, 216, 6)
     wait(back_x)
     own_d.wait()
@@ -384,12 +398,12 @@
             buf(4, 144, D), buf(3, 144, D), buf(4, 144, OW), buf(3, 144, OW),
             buf(144, OW, dtype=F32), buf(80, OW), buf(80, OW), buf(80, OW, dtype=F32),
             buf(4, 80, 128), buf(3, 80, 128),
-            buf(4, 3, 144, OW), buf(3, 3, 144, OW),
+            buf(4, 3, 144, OW), buf(3, 3, 144, OW), buf(7, 80, OW),
             buf(3, 144, OW, dtype=F32), buf(3, 80, OW), buf(3, 80, OW), buf(3, 80, OW, dtype=F32),
             buf(4, 80, 256), buf(3, 80, 256),
             dma((5,)), dma((16,)), dma((16,)), dma((3,)), dma((3,)), dma((6,)), dma((6,)),
-            dma((4,)), dma((4,)), dma((9,)), dma((9,)), dma((10,)), dma((10,)),
-            dma((3,)), dma((3,)), dma((9,)), dma((9,)), dma((3,)), dma((3,)), dma((10,)), dma((10,)),
+            dma((6,)), dma((6,)), dma((9,)), dma((9,)), dma((10,)), dma((10,)),
+            dma((3,)), dma((3,)), dma((6,)), dma((6,)), dma((7,)), dma((7,)), dma((3,)), dma((3,)), dma((10,)), dma((10,)),
         ],
         compiler_params=pltpu.CompilerParams(
             collective_id=1, has_side_effects=True, vmem_limit_bytes=56 * MIB

time: 88.1 us -> 86.6 us (0.983)
  Pallas kernels: 86.6 us -> 85.6 us
    pallas_call x1, Pallas kernels: 84.6 us -> 83.6 us  [fused(): pl.pallas_call(kernel, out_shape=[jax.ShapeDtypeStruct((16, PX, D), BF16)...]
where the time goes in v5:
time: 86.6 us; the launch traced here: 86.2 us
  Pallas kernels  85.6 us (99%)
    pallas_call x1, Pallas kernels, fused(): pl.pallas_call(kernel, out_shape=[jax.ShapeDtypeStruct((16, PX, D), BF16)...  83.6 us
    pallas_call x1, Pallas kernels, finish(): pl.pallas_call(finish_kernel, out_shape=[jax.ShapeDtypeStruct((16, PX, D)...  1.98 us

profile of v5, /device:TPU:32, one launch (start us, length us, event | category | flops | bytes accessed | tf_op | source)
XLA Modules:
  0.0 86.2 jit_solution(11984848975941218667)
XLA Ops:
  0.6 83.6 %shard_map.67 = (bf16[16,16,1152]{2,1,0:T(8,128)(2,1)}, f32[80,256]{1,0:T(8,128)}, f32[80,128]{1,0:T(8,128)}) custom-call(bf16[16,16,1152]{2,1,0:T(8,128)(2,1)} %bitcast.3, bf16[16,16,1152]{2,1,0:T(8,128)(2,1)} %bitcast.4, bf16[1152,3456]{1,0:T(8,128)(2,1)} %wqkv_hbm.1, bf16[1152,1152]{1,0:T(8,128)(2,1)} %wout_hbm.1), custom_call_target="tpu_custom_call" | custom-call | tf_op jit(solution)/shard_map/pallas_call | solution.py:383
  84.2 2.0 %shard_map.68 = (bf16[16,16,1152]{2,1,0:T(8,128)(2,1)}, f32[72,216]{1,0:T(8,128)}, f32[72,72]{1,0:T(8,128)}) custom-call(bf16[16,16,1152]{2,1,0:T(8,128)(2,1)} %get-tuple-element.9.d_x1, f32[80,256]{1,0:T(8,128)} %get-tuple-element.10.resq, f32[80,128]{1,0:T(8,128)} %get-tuple-element.11.reso), custom_call_target="tpu_custom_call" | custom-call | tf_op jit(solution)/shard_map/pallas_call | solution.py:422

commit v6 on v5

--- a/solution.py
+++ b/solution.py
@@ -411,30 +411,29 @@
     )(x, dout, wqkv, wout)
 
 
-def finish_kernel(d_x1, resq, reso, out, g_qkv, g_out):
-    out[...] = d_x1[...]
+def finish_kernel(resq, reso, g_qkv, g_out):
     g_qkv[...] = resq[0:72, 0:216] * (1.0 / 256.0)
     g_out[...] = reso[0:72, 0:72] * (1.0 / 256.0)
 
 
-def finish(d_x1, resq, reso):
+def finish(resq, reso):
     vmem = pl.BlockSpec(memory_space=pltpu.VMEM)
     return pl.pallas_call(
         finish_kernel,
         out_shape=[
-            jax.ShapeDtypeStruct((16, PX, D), BF16),
             jax.ShapeDtypeStruct((72, 216), F32),
             jax.ShapeDtypeStruct((72, 72), F32),
         ],
-        in_specs=[vmem] * 3,
-        out_specs=[vmem] * 3,
-    )(d_x1, resq, reso)
+        in_specs=[vmem] * 2,
+        out_specs=[vmem] * 2,
+    )(resq, reso)
 
 
 def local(x1_pixels, dout_frames, w_qkv, w_out):
     x = x1_pixels.reshape(FR, PX, D)
     dout = dout_frames.reshape(16, PX, D)
-    d_x1, g_qkv, g_out = finish(*fused(x, dout, w_qkv, w_out))
+    d_x1, resq, reso = fused(x, dout, w_qkv, w_out)
+    g_qkv, g_out = finish(resq, reso)
     return d_x1.reshape(dout_frames.shape), g_qkv, g_out
 
 

time: 86.6 us -> 88.2 us (1.018)
  local copies, waits for them, and re-layouts: 0 us -> 1.92 us
    unnamed x0 -> x1, local copies, waits for them, and re-layouts: none -> 1.92 us
where the time goes in v6:
time: 88.2 us; the launch traced here: 87.7 us
  Pallas kernels  85.1 us (96%)
  local copies, waits for them, and re-layouts  1.92 us (2%)
    pallas_call x1, Pallas kernels, fused(): pl.pallas_call(kernel, out_shape=[jax.ShapeDtypeStruct((16, PX, D), BF16)...  83.6 us
    unnamed x1, local copies, waits for them, and re-layouts  1.92 us

profile of v6, /device:TPU:32, one launch (start us, length us, event | category | flops | bytes accessed | tf_op | source)
XLA Modules:
  0.0 87.7 jit_solution(15101080587718459097)
XLA Ops:
  0.6 83.6 %shard_map.67 = (bf16[16,16,1152]{2,1,0:T(8,128)(2,1)}, f32[80,256]{1,0:T(8,128)}, f32[80,128]{1,0:T(8,128)}) custom-call(bf16[16,16,1152]{2,1,0:T(8,128)(2,1)} %bitcast.3, bf16[16,16,1152]{2,1,0:T(8,128)(2,1)} %bitcast.4, bf16[1152,3456]{1,0:T(8,128)(2,1)} %wqkv_hbm.1, bf16[1152,1152]{1,0:T(8,128)(2,1)} %wout_hbm.1), custom_call_target="tpu_custom_call" | custom-call | tf_op jit(solution)/shard_map/pallas_call | solution.py:383
  84.2 1.5 %shard_map.68 = (f32[72,216]{1,0:T(8,128)}, f32[72,72]{1,0:T(8,128)}) custom-call(f32[80,256]{1,0:T(8,128)} %get-tuple-element.9.resq, f32[80,128]{1,0:T(8,128)} %get-tuple-element.10.reso), custom_call_target="tpu_custom_call" | custom-call | tf_op jit(solution)/shard_map/pallas_call | solution.py:421
  85.8 1.9 %copy.8 = bf16[1,1,256,1152]{3,2,1,0:T(8,128)(2,1)} copy(bf16[1,1,256,1152]{3,2,1,0:T(8,128)(2,1)} %bitcast.5) | data formatting | bytes 1179648
